TPU v7x, 32 devices: a whole 2x2x4 slice. The times are simulated.
32 devices in a mesh: table: 4 (over y, core), rows: 8 (over z, x).
Axes of the slice: x: 2, y: 2, z: 4, core: 2. Of those that a mesh axis runs over, the one named last changes fastest.
Arguments:
- cells: bfloat16 [4, 512, 119, 192], P('table', 'rows'), may hold values from -6 to 6
- cotangent: bfloat16 [4, 512, 119, 192], P('table', 'rows'), may hold values from -6 to 6
- train_count: int32 [4], P('table'), may hold values from 8 to 32
- key_mask: int32 [4, 32], P('table', 'rows'), may hold values 0 or 1
- train_order: int32 [4, 32], P('table', 'rows'), may hold values from 0 to 31, each once within a row
- proj_weights: float32 [6, 192, 192], replicated, may hold values from -0.4375 to 0.4375
- out_weights: float32 [2, 192, 192], replicated
- mlp_in: float32 [192, 768], replicated, may hold values from -0.4375 to 0.4375
- mlp_out: float32 [768, 192], replicated, may hold values from -0.21875 to 0.21875
- norm_params: float32 [6, 192], replicated
- square_rows: float32 [8, 192], replicated, may hold values from 2437.12 to 9748.48
- square_cols: float32 [8, 192], replicated, may hold values from 2437.12 to 9748.48
- mlp_model_stats: float32 [2, 192], replicated, may hold values from 24371.2 to 97484.8
- mlp_hidden_stats: float32 [2, 768], replicated, may hold values from 24371.2 to 97484.8
- norm_second: float32 [6, 192], replicated, may hold values from 24371.2 to 97484.8
Outputs:
- out_cells: bfloat16 [4, 512, 119, 192], P('table', 'rows')
- cells_grad: float32 [4, 512, 119, 192], P('table', 'rows')
- proj_grad: float32 [6, 192, 192], replicated
- out_grad: float32 [2, 192, 192], replicated
- mlp_in_grad: float32 [192, 768], replicated
- mlp_out_grad: float32 [768, 192], replicated
- norm_grad: float32 [6, 192], replicated
- proj_new: float32 [6, 192, 192], replicated
- out_new: float32 [2, 192, 192], replicated
- mlp_in_new: float32 [192, 768], replicated
- mlp_out_new: float32 [768, 192], replicated
- norm_new: float32 [6, 192], replicated
- square_rows_new: float32 [8, 192], replicated
- square_cols_new: float32 [8, 192], replicated
- mlp_model_new: float32 [2, 192], replicated
- mlp_hidden_new: float32 [2, 768], replicated
- norm_second_new: float32 [6, 192], replicated
All inputs are finite; a program needn't handle non-finite values. No bound on the sum of `key_mask` on one device may be relied on, other than what follows from the above.
Results may differ from a plain program's by a relative error of at most 0.024.
Values may be sent and summed in bfloat16 or wider, within the bound.
No kernel may reach another device: no remote copies, remote signals or barrier semaphores. Data moves between devices by JAX's collectives and lax.ppermute only.
A program may use at most 768 MiB of HBM per device.

v0:
```python
import jax
import jax.numpy as jnp
from jax import lax
from jax.sharding import PartitionSpec as P

HEADS = 6
HEAD = 32
FEAT_BLOCK = 17
STEP = 3


CLIP = 0.3
RATE = 0.5


def split_heads(value):
    return value.reshape(value.shape[:-1] + (HEADS, HEAD))


def product(left, right):
    return jnp.dot(left, right, preferred_element_type=jnp.float32)


def outer_sum(operand, gradient):
    return jnp.einsum("rfd,rfe->de", operand, gradient, preferred_element_type=jnp.float32)


def layer_norm(value, gain, shift):
    center = value - jnp.mean(value, -1, keepdims=True)
    recip = lax.rsqrt(jnp.mean(center * center, -1, keepdims=True) + 1e-05)
    normed = center * recip
    return (normed * gain + shift, normed, recip)


def norm_back(gradient, normed, recip, gain):
    scaled = gradient * gain
    inner = (
        scaled
        - jnp.mean(scaled, -1, keepdims=True)
        - normed * jnp.mean(scaled * normed, -1, keepdims=True)
    )
    return (inner * recip, jnp.sum(gradient * normed, axis=(0, 1)), jnp.sum(gradient, axis=(0, 1)))


def item_scores(queries, slot_keys, usable, score_scale):
    scores = (
        jnp.einsum(
            "rfhe,kfhe->fhrk",
            split_heads(queries),
            split_heads(slot_keys),
            preferred_element_type=jnp.float32,
        )
        * score_scale
    )
    return jnp.where(usable[None, None, None, :] > 0, scores, -1e30)


def factored_step(grad, rows_old, cols_old, weight):
    decay = 1.0 - STEP ** (-0.8)
    square = grad * grad + 1e-30
    rows_new = decay * rows_old + (1.0 - decay) * jnp.mean(square, -1)
    cols_new = decay * cols_old + (1.0 - decay) * jnp.mean(square, -2)
    estimate = (
        rows_new[..., :, None] * cols_new[..., None, :] / jnp.mean(rows_new, -1)[..., None, None]
    )
    update = grad * lax.rsqrt(estimate)
    update_rms = jnp.sqrt(jnp.mean(update * update, (-2, -1), keepdims=True))
    update = update / jnp.maximum(1.0, update_rms / CLIP)
    weight_rms = jnp.sqrt(jnp.mean(weight * weight, (-2, -1), keepdims=True))
    return (weight - RATE * jnp.maximum(0.001, weight_rms) * update, rows_new, cols_new)


def vector_step(grad, second_old, param):
    decay = 1.0 - STEP ** (-0.8)
    second_new = decay * second_old + (1.0 - decay) * (grad * grad + 1e-30)
    update = grad * lax.rsqrt(second_new)
    update_rms = jnp.sqrt(jnp.mean(update * update, -1, keepdims=True))
    update = update / jnp.maximum(1.0, update_rms / CLIP)
    param_rms = jnp.sqrt(jnp.mean(param * param, -1, keepdims=True))
    return (param - RATE * jnp.maximum(0.001, param_rms) * update, second_new)


def on_device(
    cells,
    cotangent,
    train_count,
    key_mask,
    train_order,
    proj_weights,
    out_weights,
    mlp_in,
    mlp_out,
    norm_params,
    square_rows,
    square_cols,
    mlp_model_stats,
    mlp_hidden_stats,
    norm_second,
):
    bf16 = jnp.bfloat16
    f32 = jnp.float32
    score_scale = HEAD ** (-0.5)
    inputs = cells[0]
    inputs_f = inputs.astype(f32)
    rows_here = inputs.shape[0]
    feats = inputs.shape[1]
    slots_here = key_mask.shape[1]
    width = FEAT_BLOCK
    proj_low = proj_weights.astype(bf16)
    outw_low = out_weights.astype(bf16)
    in_low = mlp_in.astype(bf16)
    hid_low = mlp_out.astype(bf16)
    order_here = train_order[0]
    usable = (order_here < train_count[0]) & ((key_mask[0] == 1) | (order_here == 0))
    usable_low = usable.astype(bf16)
    query_feat = product(inputs, proj_low[0]).astype(bf16)
    key_feat = product(inputs, proj_low[1]).astype(bf16)
    value_feat = product(inputs, proj_low[2]).astype(bf16)
    feat_scores = (
        jnp.einsum(
            "rfhe,rghe->rhfg",
            split_heads(query_feat),
            split_heads(key_feat),
            preferred_element_type=f32,
        )
        * score_scale
    )
    feat_max = jnp.max(feat_scores, -1, keepdims=True)
    feat_exp = jnp.exp(feat_scores - feat_max)
    feat_probs = feat_exp / jnp.sum(feat_exp, -1, keepdims=True)
    feat_probs_low = feat_probs.astype(bf16)
    out_feat = jnp.einsum(
        "rhfg,rghe->rfhe", feat_probs_low, split_heads(value_feat), preferred_element_type=f32
    )
    out_feat = out_feat.reshape(inputs.shape).astype(bf16)
    hidden_one, normed_one, recip_one = layer_norm(
        inputs_f + product(out_feat, outw_low[0]), norm_params[0], norm_params[1]
    )
    hidden_one_low = hidden_one.astype(bf16)
    query_item = product(hidden_one_low, proj_low[3]).astype(bf16)
    train_low = hidden_one_low[:slots_here]
    key_item = product(train_low, proj_low[4]).astype(bf16)
    value_item = product(train_low, proj_low[5]).astype(bf16)
    out_parts = []
    lse_parts = []
    for block in range(feats // width):
        columns = slice(block * width, (block + 1) * width)
        keys_all, values_all, usable_all = (
            lax.all_gather(key_item[:, columns], "rows", axis=0, tiled=True),
            lax.all_gather(value_item[:, columns], "rows", axis=0, tiled=True),
            lax.all_gather(usable_low, "rows", axis=0, tiled=True),
        )
        scores = item_scores(query_item[:, columns], keys_all, usable_all, score_scale)
        row_max = jnp.max(scores, -1, keepdims=True)
        expon = jnp.exp(scores - row_max)
        total = jnp.sum(expon, -1, keepdims=True)
        lse_parts.append((row_max + jnp.log(total))[..., 0])
        probs_low = (expon / total).astype(bf16)
        block_out = jnp.einsum(
            "fhrk,kfhe->rfhe", probs_low, split_heads(values_all), preferred_element_type=f32
        )
        out_parts.append(block_out.reshape(rows_here, width, -1).astype(bf16))
    out_item = jnp.concatenate(out_parts, 1)
    hidden_two, normed_two, recip_two = layer_norm(
        hidden_one + product(out_item, outw_low[1]), norm_params[2], norm_params[3]
    )
    hidden_two_low = hidden_two.astype(bf16)
    pre_act = product(hidden_two_low, in_low)
    activ, gelu_pull = jax.vjp(jax.nn.gelu, pre_act)
    activ_low = activ.astype(bf16)
    result, normed_three, recip_three = layer_norm(
        hidden_two + product(activ_low, hid_low), norm_params[4], norm_params[5]
    )
    grad_out = cotangent[0].astype(f32)
    grad_three, gain_three, shift_three = norm_back(
        grad_out, normed_three, recip_three, norm_params[4]
    )
    branch_grad = grad_three.astype(bf16)
    hid_grad = jnp.einsum("rfk,rfd->kd", activ_low, branch_grad, preferred_element_type=f32)
    act_grad = product(branch_grad, hid_low.T)
    pre_grad = gelu_pull(act_grad)[0].astype(bf16)
    in_grad = jnp.einsum("rfd,rfk->dk", hidden_two_low, pre_grad, preferred_element_type=f32)
    grad_hidden_two = grad_three + product(pre_grad, in_low.T)
    grad_two, gain_two, shift_two = norm_back(
        grad_hidden_two, normed_two, recip_two, norm_params[2]
    )
    item_branch_grad = grad_two.astype(bf16)
    out_item_weight_grad = outer_sum(out_item, item_branch_grad)
    out_item_grad = product(item_branch_grad, outw_low[1].T).astype(bf16)
    query_grad_parts = []
    key_grad_parts = []
    value_grad_parts = []
    for block in range(feats // width):
        columns = slice(block * width, (block + 1) * width)
        keys_all, values_all, usable_all = (
            lax.all_gather(key_item[:, columns], "rows", axis=0, tiled=True),
            lax.all_gather(value_item[:, columns], "rows", axis=0, tiled=True),
            lax.all_gather(usable_low, "rows", axis=0, tiled=True),
        )
        query_block = query_item[:, columns]
        grad_block = out_item_grad[:, columns]
        lse_block = lse_parts[block]
        probs = jnp.exp(
            item_scores(query_block, keys_all, usable_all, score_scale) - lse_block[..., None]
        )
        prob_grad = jnp.einsum(
            "rfhe,kfhe->fhrk",
            split_heads(grad_block),
            split_heads(values_all),
            preferred_element_type=f32,
        )
        offset = jnp.sum(probs * prob_grad, -1)
        score_grad = (probs * (prob_grad - offset[..., None])).astype(bf16)
        query_grad = (
            jnp.einsum(
                "fhrk,kfhe->rfhe", score_grad, split_heads(keys_all), preferred_element_type=f32
            )
            * score_scale
        )
        query_grad_parts.append(query_grad.reshape(rows_here, width, -1))
        queries_all, grads_all = (
            lax.all_gather(query_block, "rows", axis=0, tiled=True),
            lax.all_gather(grad_block, "rows", axis=0, tiled=True),
        )
        lse_all, offset_all = (
            lax.all_gather(lse_block.astype(jnp.bfloat16), "rows", axis=2, tiled=True).astype(
                lse_block.dtype
            ),
            lax.all_gather(offset.astype(jnp.bfloat16), "rows", axis=2, tiled=True).astype(
                offset.dtype
            ),
        )
        own_probs = jnp.exp(
            item_scores(queries_all, key_item[:, columns], usable_low, score_scale)
            - lse_all[..., None]
        )
        own_prob_grad = jnp.einsum(
            "rfhe,kfhe->fhrk",
            split_heads(grads_all),
            split_heads(value_item[:, columns]),
            preferred_element_type=f32,
        )
        own_score_grad = (own_probs * (own_prob_grad - offset_all[..., None])).astype(bf16)
        key_block = (
            jnp.einsum(
                "fhrk,rfhe->kfhe",
                own_score_grad,
                split_heads(queries_all),
                preferred_element_type=f32,
            )
            * score_scale
        )
        value_block = jnp.einsum(
            "fhrk,rfhe->kfhe",
            own_probs.astype(bf16),
            split_heads(grads_all),
            preferred_element_type=f32,
        )
        key_block = key_block.reshape(slots_here, width, -1)
        value_block = value_block.reshape(slots_here, width, -1)
        key_grad_parts.append(key_block)
        value_grad_parts.append(value_block)
    query_item_grad = jnp.concatenate(query_grad_parts, 1).astype(bf16)
    key_item_grad = jnp.concatenate(key_grad_parts, 1).astype(bf16)
    value_item_grad = jnp.concatenate(value_grad_parts, 1).astype(bf16)
    grad_hidden_one = grad_two + product(query_item_grad, proj_low[3].T)
    slot_back = product(key_item_grad, proj_low[4].T) + product(value_item_grad, proj_low[5].T)
    grad_hidden_one = jnp.concatenate(
        [grad_hidden_one[:slots_here] + slot_back, grad_hidden_one[slots_here:]], 0
    )
    grad_one, gain_one, shift_one = norm_back(
        grad_hidden_one, normed_one, recip_one, norm_params[0]
    )
    feat_branch_grad = grad_one.astype(bf16)
    out_feat_weight_grad = outer_sum(out_feat, feat_branch_grad)
    out_feat_grad = product(feat_branch_grad, outw_low[0].T).astype(bf16)
    feat_prob_grad = jnp.einsum(
        "rfhe,rghe->rhfg",
        split_heads(out_feat_grad),
        split_heads(value_feat),
        preferred_element_type=f32,
    )
    feat_offset = jnp.sum(feat_probs * feat_prob_grad, -1, keepdims=True)
    feat_score_grad = (feat_probs * (feat_prob_grad - feat_offset)).astype(bf16)
    query_feat_grad = (
        (
            jnp.einsum(
                "rhfg,rghe->rfhe",
                feat_score_grad,
                split_heads(key_feat),
                preferred_element_type=f32,
            )
            * score_scale
        )
        .reshape(inputs.shape)
        .astype(bf16)
    )
    key_feat_grad = (
        (
            jnp.einsum(
                "rhfg,rfhe->rghe",
                feat_score_grad,
                split_heads(query_feat),
                preferred_element_type=f32,
            )
            * score_scale
        )
        .reshape(inputs.shape)
        .astype(bf16)
    )
    value_feat_grad = (
        jnp.einsum(
            "rhfg,rfhe->rghe",
            feat_probs_low,
            split_heads(out_feat_grad),
            preferred_element_type=f32,
        )
        .reshape(inputs.shape)
        .astype(bf16)
    )
    cells_grad = (
        grad_one
        + product(query_feat_grad, proj_low[0].T)
        + product(key_feat_grad, proj_low[1].T)
        + product(value_feat_grad, proj_low[2].T)
    )
    proj_grad = jnp.stack(
        [
            outer_sum(inputs, query_feat_grad),
            outer_sum(inputs, key_feat_grad),
            outer_sum(inputs, value_feat_grad),
            outer_sum(hidden_one_low, query_item_grad),
            outer_sum(train_low, key_item_grad),
            outer_sum(train_low, value_item_grad),
        ]
    )
    out_grad = jnp.stack([out_feat_weight_grad, out_item_weight_grad])
    norm_grad = jnp.stack([gain_one, shift_one, gain_two, shift_two, gain_three, shift_three])
    proj_sum, out_sum, in_sum, hid_sum, norm_sum = lax.psum(
        (proj_grad, out_grad, in_grad, hid_grad, norm_grad), ("table", "rows")
    )
    proj_new, proj_rows, proj_cols = factored_step(
        proj_sum, square_rows[:6], square_cols[:6], proj_weights
    )
    out_new, out_rows, out_cols = factored_step(
        out_sum, square_rows[6:], square_cols[6:], out_weights
    )
    in_new, in_rows, in_cols = factored_step(
        in_sum, mlp_model_stats[0], mlp_hidden_stats[0], mlp_in
    )
    hid_new, hid_rows, hid_cols = factored_step(
        hid_sum, mlp_hidden_stats[1], mlp_model_stats[1], mlp_out
    )
    norm_new, second_new = vector_step(norm_sum, norm_second, norm_params)
    rows_new = jnp.concatenate([proj_rows, out_rows], 0)
    cols_new = jnp.concatenate([proj_cols, out_cols], 0)
    model_new = jnp.stack([in_rows, hid_cols])
    hidden_new = jnp.stack([in_cols, hid_rows])
    return (
        result.astype(bf16)[None],
        cells_grad[None],
        proj_sum,
        out_sum,
        in_sum,
        hid_sum,
        norm_sum,
        proj_new,
        out_new,
        in_new,
        hid_new,
        norm_new,
        rows_new,
        cols_new,
        model_new,
        hidden_new,
        second_new,
    )


def solution(mesh):
    return jax.shard_map(
        on_device,
        mesh=mesh,
        in_specs=(
            P("table", "rows", None, None),
            P("table", "rows", None, None),
            P("table"),
            P("table", "rows"),
            P("table", "rows"),
            P(),
            P(),
            P(),
            P(),
            P(),
            P(),
            P(),
            P(),
            P(),
            P(),
        ),
        out_specs=(
            P("table", "rows", None, None),
            P("table", "rows", None, None),
            P(),
            P(),
            P(),
            P(),
            P(),
            P(),
            P(),
            P(),
            P(),
            P(),
            P(),
            P(),
            P(),
            P(),
            P(),
        ),
        check_vma=False,
    )
```

profile of v0, /device:TPU:0, one launch (start us, length us, event | category | flops | bytes accessed | tf_op | source)
XLA Modules:
  0.0 2397.2 jit_solution(567461934883549620)
XLA Ops:
  21.0 17.1 fusion.259
  38.1 13.7 fusion.53
  62.5 9.5 fusion.255
  82.5 24.4 %all-reduce = bf16[32]{0:T(256)(128)(2,1)} all-reduce(bf16[32]{0:T(256)(128)(2,1)S(1)} %dynamic-update-slice), channel_id=2, replica_groups=mesh['table'=4,'rows'=8] {'rows'}, use_global_device_ids=true, to_apply=%add | all-reduce | flops 32 | bytes 128
  118.5 34.7 %all_gather.158 = bf16[32,17,192]{2,1,0:T(8,128)(2,1)} all-gather(bf16[4,17,192]{2,1,0:T(8,128)(2,1)} %copy.872), channel_id=1, replica_groups=mesh['table'=4,'rows'=8] {'rows'}, dimensions={0}, use_global_device_ids=true | all-gather | bytes 235008 | tf_op jit(solution)/shard_map/all_gather | solution.py:149
  153.1 33.8 %all_gather.160 = bf16[32,17,192]{2,1,0:T(8,128)(2,1)} all-gather(bf16[4,17,192]{2,1,0:T(8,128)(2,1)} %copy.878), channel_id=1, replica_groups=mesh['table'=4,'rows'=8] {'rows'}, dimensions={0}, use_global_device_ids=true | all-gather | bytes 235008 | tf_op jit(solution)/shard_map/all_gather | solution.py:149
  187.0 33.2 %all_gather.162 = bf16[32,17,192]{2,1,0:T(8,128)(2,1)} all-gather(bf16[4,17,192]{2,1,0:T(8,128)(2,1)} %copy.884), channel_id=1, replica_groups=mesh['table'=4,'rows'=8] {'rows'}, dimensions={0}, use_global_device_ids=true | all-gather | bytes 235008 | tf_op jit(solution)/shard_map/all_gather | solution.py:149
  220.2 33.0 %all_gather.164 = bf16[32,17,192]{2,1,0:T(8,128)(2,1)} all-gather(bf16[4,17,192]{2,1,0:T(8,128)(2,1)S(1)} %copy.890), channel_id=1, replica_groups=mesh['table'=4,'rows'=8] {'rows'}, dimensions={0}, use_global_device_ids=true | all-gather | bytes 235008 | tf_op jit(solution)/shard_map/all_gather | solution.py:149
  253.2 33.1 %all_gather.166 = bf16[32,17,192]{2,1,0:T(8,128)(2,1)} all-gather(bf16[4,17,192]{2,1,0:T(8,128)(2,1)S(1)} %copy.896), channel_id=1, replica_groups=mesh['table'=4,'rows'=8] {'rows'}, dimensions={0}, use_global_device_ids=true | all-gather | bytes 235008 | tf_op jit(solution)/shard_map/all_gather | solution.py:149
  286.3 33.1 %all_gather.168 = bf16[32,17,192]{2,1,0:T(8,128)(2,1)} all-gather(bf16[4,17,192]{2,1,0:T(8,128)(2,1)S(1)} %copy.902), channel_id=1, replica_groups=mesh['table'=4,'rows'=8] {'rows'}, dimensions={0}, use_global_device_ids=true | all-gather | bytes 235008 | tf_op jit(solution)/shard_map/all_gather | solution.py:149
  319.4 33.1 %all_gather.170 = bf16[32,17,192]{2,1,0:T(8,128)(2,1)} all-gather(bf16[4,17,192]{2,1,0:T(8,128)(2,1)S(1)} %copy.908), channel_id=1, replica_groups=mesh['table'=4,'rows'=8] {'rows'}, dimensions={0}, use_global_device_ids=true | all-gather | bytes 235008 | tf_op jit(solution)/shard_map/all_gather | solution.py:149
  378.1 33.4 %all_gather.156 = bf16[32,17,192]{2,1,0:T(8,128)(2,1)} all-gather(bf16[4,17,192]{2,1,0:T(8,128)(2,1)} %copy.870), channel_id=1, replica_groups=mesh['table'=4,'rows'=8] {'rows'}, dimensions={0}, use_global_device_ids=true | all-gather | bytes 235008 | tf_op jit(solution)/shard_map/all_gather | solution.py:150
  411.4 33.4 %all_gather.159 = bf16[32,17,192]{2,1,0:T(8,128)(2,1)} all-gather(bf16[4,17,192]{2,1,0:T(8,128)(2,1)} %copy.876), channel_id=1, replica_groups=mesh['table'=4,'rows'=8] {'rows'}, dimensions={0}, use_global_device_ids=true | all-gather | bytes 235008 | tf_op jit(solution)/shard_map/all_gather | solution.py:150
  444.8 33.5 %all_gather.161 = bf16[32,17,192]{2,1,0:T(8,128)(2,1)} all-gather(bf16[4,17,192]{2,1,0:T(8,128)(2,1)} %copy.882), channel_id=1, replica_groups=mesh['table'=4,'rows'=8] {'rows'}, dimensions={0}, use_global_device_ids=true | all-gather | bytes 235008 | tf_op jit(solution)/shard_map/all_gather | solution.py:150
  478.3 33.0 %all_gather.163 = bf16[32,17,192]{2,1,0:T(8,128)(2,1)} all-gather(bf16[4,17,192]{2,1,0:T(8,128)(2,1)S(1)} %copy.888), channel_id=1, replica_groups=mesh['table'=4,'rows'=8] {'rows'}, dimensions={0}, use_global_device_ids=true | all-gather | bytes 235008 | tf_op jit(solution)/shard_map/all_gather | solution.py:150
  511.3 33.1 %all_gather.165 = bf16[32,17,192]{2,1,0:T(8,128)(2,1)} all-gather(bf16[4,17,192]{2,1,0:T(8,128)(2,1)S(1)} %copy.894), channel_id=1, replica_groups=mesh['table'=4,'rows'=8] {'rows'}, dimensions={0}, use_global_device_ids=true | all-gather | bytes 235008 | tf_op jit(solution)/shard_map/all_gather | solution.py:150
  544.3 33.0 %all_gather.167 = bf16[32,17,192]{2,1,0:T(8,128)(2,1)} all-gather(bf16[4,17,192]{2,1,0:T(8,128)(2,1)S(1)} %copy.900), channel_id=1, replica_groups=mesh['table'=4,'rows'=8] {'rows'}, dimensions={0}, use_global_device_ids=true | all-gather | bytes 235008 | tf_op jit(solution)/shard_map/all_gather | solution.py:150
  577.3 33.0 %all_gather.169 = bf16[32,17,192]{2,1,0:T(8,128)(2,1)} all-gather(bf16[4,17,192]{2,1,0:T(8,128)(2,1)S(1)} %copy.906), channel_id=1, replica_groups=mesh['table'=4,'rows'=8] {'rows'}, dimensions={0}, use_global_device_ids=true | all-gather | bytes 235008 | tf_op jit(solution)/shard_map/all_gather | solution.py:150
  698.2 6.4 copy.916
  720.3 19.1 concatenate.24
  746.8 10.0 fusion.222
  756.8 16.5 fusion.269
  777.9 6.5 fusion.22
  784.4 22.8 fusion.7
  807.2 12.7 multiply_reduce_fusion.2
  828.7 9.8 fusion.254
  909.9 15.7 fusion.110
  962.9 37.4 %all_gather.172 = bf16[17,6,512]{0,1,2:T(8,128)(2,1)} all-gather(bf16[17,6,64]{0,1,2:T(8,128)(2,1)S(1)} %copy.952), channel_id=1, replica_groups=mesh['table'=4,'rows'=8] {'rows'}, dimensions={2}, use_global_device_ids=true | all-gather | bytes 117504 | tf_op jit(solution)/shard_map/all_gather | solution.py:226
  1003.1 37.5 %all_gather.176 = bf16[17,6,512]{0,1,2:T(8,128)(2,1)} all-gather(bf16[17,6,64]{0,1,2:T(8,128)(2,1)} %copy.963), channel_id=1, replica_groups=mesh['table'=4,'rows'=8] {'rows'}, dimensions={2}, use_global_device_ids=true | all-gather | bytes 117504 | tf_op jit(solution)/shard_map/all_gather | solution.py:226
  1043.3 37.6 %all_gather.180 = bf16[17,6,512]{0,1,2:T(8,128)(2,1)} all-gather(bf16[17,6,64]{0,1,2:T(8,128)(2,1)} %copy.974), channel_id=1, replica_groups=mesh['table'=4,'rows'=8] {'rows'}, dimensions={2}, use_global_device_ids=true | all-gather | bytes 117504 | tf_op jit(solution)/shard_map/all_gather | solution.py:226
  1083.7 37.8 %all_gather.184 = bf16[17,6,512]{0,1,2:T(8,128)(2,1)} all-gather(bf16[17,6,64]{0,1,2:T(8,128)(2,1)} %copy.985), channel_id=1, replica_groups=mesh['table'=4,'rows'=8] {'rows'}, dimensions={2}, use_global_device_ids=true | all-gather | bytes 117504 | tf_op jit(solution)/shard_map/all_gather | solution.py:226
  1124.3 36.8 %all_gather.188 = bf16[17,6,512]{0,1,2:T(8,128)(2,1)} all-gather(bf16[17,6,64]{0,1,2:T(8,128)(2,1)} %copy.996), channel_id=1, replica_groups=mesh['table'=4,'rows'=8] {'rows'}, dimensions={2}, use_global_device_ids=true | all-gather | bytes 117504 | tf_op jit(solution)/shard_map/all_gather | solution.py:226
  1163.8 36.9 %all_gather.192 = bf16[17,6,512]{0,1,2:T(8,128)(2,1)} all-gather(bf16[17,6,64]{0,1,2:T(8,128)(2,1)S(1)} %copy.1007), channel_id=1, replica_groups=mesh['table'=4,'rows'=8] {'rows'}, dimensions={2}, use_global_device_ids=true | all-gather | bytes 117504 | tf_op jit(solution)/shard_map/all_gather | solution.py:226
  1203.5 38.0 %all_gather.196 = bf16[17,6,512]{0,1,2:T(8,128)(2,1)} all-gather(bf16[17,6,64]{0,1,2:T(8,128)(2,1)S(1)} %copy.1018), channel_id=1, replica_groups=mesh['table'=4,'rows'=8] {'rows'}, dimensions={2}, use_global_device_ids=true | all-gather | bytes 117504 | tf_op jit(solution)/shard_map/all_gather | solution.py:226
  1319.7 35.0 %all_gather.198 = bf16[17,6,512]{0,1,2:T(8,128)(2,1)S(1)} all-gather(bf16[17,6,64]{0,1,2:T(8,128)(2,1)S(1)} %copy.1023), channel_id=1, replica_groups=mesh['table'=4,'rows'=8] {'rows'}, dimensions={2}, use_global_device_ids=true | all-gather | bytes 117504 | tf_op jit(solution)/shard_map/all_gather | solution.py:229
  1356.3 35.9 %all_gather.194 = bf16[17,6,512]{0,1,2:T(8,128)(2,1)S(1)} all-gather(bf16[17,6,64]{0,1,2:T(8,128)(2,1)S(1)} %copy-done.134), channel_id=1, replica_groups=mesh['table'=4,'rows'=8] {'rows'}, dimensions={2}, use_global_device_ids=true | all-gather | bytes 117504 | tf_op jit(solution)/shard_map/all_gather | solution.py:229
  1393.8 34.5 %all_gather.190 = bf16[17,6,512]{0,1,2:T(8,128)(2,1)S(1)} all-gather(bf16[17,6,64]{0,1,2:T(8,128)(2,1)S(1)} %copy-done.133), channel_id=1, replica_groups=mesh['table'=4,'rows'=8] {'rows'}, dimensions={2}, use_global_device_ids=true | all-gather | bytes 117504 | tf_op jit(solution)/shard_map/all_gather | solution.py:229
  1429.9 34.3 %all_gather.186 = bf16[17,6,512]{0,1,2:T(8,128)(2,1)S(1)} all-gather(bf16[17,6,64]{0,1,2:T(8,128)(2,1)S(1)} %copy-done.132), channel_id=1, replica_groups=mesh['table'=4,'rows'=8] {'rows'}, dimensions={2}, use_global_device_ids=true | all-gather | bytes 117504 | tf_op jit(solution)/shard_map/all_gather | solution.py:229
  1465.8 35.6 %all_gather.182 = bf16[17,6,512]{0,1,2:T(8,128)(2,1)S(1)} all-gather(bf16[17,6,64]{0,1,2:T(8,128)(2,1)S(1)} %copy-done.131), channel_id=1, replica_groups=mesh['table'=4,'rows'=8] {'rows'}, dimensions={2}, use_global_device_ids=true | all-gather | bytes 117504 | tf_op jit(solution)/shard_map/all_gather | solution.py:229
  1503.0 34.8 %all_gather.178 = bf16[17,6,512]{0,1,2:T(8,128)(2,1)S(1)} all-gather(bf16[17,6,64]{0,1,2:T(8,128)(2,1)S(1)} %copy.968), channel_id=1, replica_groups=mesh['table'=4,'rows'=8] {'rows'}, dimensions={2}, use_global_device_ids=true | all-gather | bytes 117504 | tf_op jit(solution)/shard_map/all_gather | solution.py:229
  1539.4 6.6 copy.947
  1546.0 7.0 copy.946
  1553.0 6.9 copy.945
  1559.9 6.9 copy.944
  1566.8 6.9 copy.943
  1573.8 6.9 copy.942
  1580.7 6.9 copy.941
  1587.6 19.8 concatenate.25
  1617.2 36.9 %all_gather.174 = bf16[17,6,512]{0,1,2:T(8,128)(2,1)} all-gather(bf16[17,6,64]{0,1,2:T(8,128)(2,1)S(1)} %copy.957), channel_id=1, replica_groups=mesh['table'=4,'rows'=8] {'rows'}, dimensions={2}, use_global_device_ids=true | all-gather | bytes 117504 | tf_op jit(solution)/shard_map/all_gather | solution.py:229
  1658.1 10.2 convolution_bitcast_fusion
  1757.3 14.6 all-gather.20.cloned.1.call-done
  1778.1 70.7 %all-gather.22.cloned.1.call-done = bf16[512,17,192]{2,0,1:T(8,128)(2,1)} async-done(((bf16[64,17,192]{2,0,1:T(8,128)(2,1)}), bf16[512,17,192]{2,0,1:T(8,128)(2,1)}) %all-gather.22.cloned.1.call-update) | async-done | bytes 3342352 | tf_op jit(solution)/shard_map/all_gather | solution.py:223
  1860.7 65.8 %all-gather.16.cloned.1.call-done = bf16[512,17,192]{2,0,1:T(8,128)(2,1)} async-done(((bf16[64,17,192]{2,0,1:T(8,128)(2,1)}), bf16[512,17,192]{2,0,1:T(8,128)(2,1)}) %all-gather.16.cloned.1.call-update) | async-done | bytes 3342352 | tf_op jit(solution)/shard_map/all_gather | solution.py:222
  1936.4 66.9 %all-gather.18.cloned.1.call-done = bf16[512,17,192]{2,0,1:T(8,128)(2,1)} async-done(((bf16[64,17,192]{2,0,1:T(8,128)(2,1)}), bf16[512,17,192]{2,0,1:T(8,128)(2,1)}) %all-gather.18.cloned.1.call-update) | async-done | bytes 3342352 | tf_op jit(solution)/shard_map/all_gather | solution.py:223
  2003.4 6.6 copy.955
  2063.3 8.9 multiply_reduce_fusion.3
  2080.3 12.3 fusion.56
  2092.6 16.9 multiply_reduce_fusion
  2109.5 20.5 multiply_convert_fusion
  2130.1 10.4 multiply_convert_fusion.2
  2140.5 8.7 multiply_convert_fusion.3
  2156.8 38.8 %psum.39 = f32[6,192]{1,0:T(8,128)S(1)} all-reduce(f32[6,192]{1,0:T(8,128)S(1)} %stack.74), channel_id=1, replica_groups=mesh['table'=4,'rows'=8] {'table','rows'}, use_global_device_ids=true, to_apply=%region_47.48 | all-reduce | flops 1152 | bytes 9216 | tf_op jit(solution)/shard_map/psum | solution.py:339
  2212.1 11.1 add_bitcast_fusion
  2223.2 126.9 %all-reduce.4.cloned.1.call-done = (f32[6,192,192]{1,2,0:T(8,128)}, f32[2,192,192]{2,1,0:T(8,128)}, f32[192,768]{1,0:T(8,128)}, f32[768,192]{0,1:T(8,128)}) async-done(((f32[6,192,192]{1,2,0:T(8,128)}, f32[2,192,192]{2,1,0:T(8,128)}, f32[192,768]{1,0:T(8,128)}, f32[768,192]{0,1:T(8,128)}), (f32[6,192,192]{1,2,0:T(8,128)}, f32[2,192,192]{2,1,0:T(8,128)}, f32[192,768]{1,0:T(8,128)}, ...) | async-done | bytes 2359312 | tf_op jit(solution)/shard_map/psum | solution.py:339
  (776 shorter events, 658.5 us)
Async XLA Ops:
  7.2 1661.1 %all-gather.40.cloned.1.call-start = ((), (), s32[]{:S(2)}) async-start(), calls=%async_computation.12 | async-start | bytes 5013504 | tf_op jit(solution)/shard_map/all_gather | solution.py:222
  20.2 719.3 %copy-start.179 = (f32[1,192]{1,0:T(1,128)}, f32[1,192]{1,0:T(1,128)S(1)}, u32[]{:S(2)}) copy-start(f32[1,192]{1,0:T(1,128)S(1)} %get-tuple-element.205) | copy-start | bytes 2308
  38.1 13.7 copy-start.93
  72.0 553.0 %copy-start.16 = (bf16[64,17,192]{1,2,0:T(8,128)(2,1)}, bf16[64,17,192]{1,2,0:T(8,128)(2,1)S(1)}, u32[]{:S(2)}) copy-start(bf16[64,17,192]{1,2,0:T(8,128)(2,1)S(1)} %get-tuple-element.185) | copy-start | bytes 1253380
  77.3 1597.3 %all-gather.42.cloned.1.call-start = ((), (), s32[]{:S(2)}) async-start(), calls=%async_computation.13 | async-start | bytes 5013504 | tf_op jit(solution)/shard_map/all_gather | solution.py:223
  369.6 245.1 %copy-start.98 = (bf16[4,17,192]{1,2,0:T(8,128)(2,1)}, bf16[4,17,192]{1,2,0:T(8,128)(2,1)S(1)}, u32[]{:S(2)}) copy-start(bf16[4,17,192]{1,2,0:T(8,128)(2,1)S(1)} %get-tuple-element.193) | copy-start | bytes 78340
  720.3 19.1 copy-start.94
  720.3 19.1 copy-start.103
  720.3 19.1 copy-start.107
  745.3 74.7 %copy-start.5 = (f32[64,119,192]{1,2,0:T(8,128)}, f32[64,119,192]{1,2,0:T(8,128)S(1)}, u32[]{:S(2)}) copy-start(f32[64,119,192]{1,2,0:T(8,128)S(1)} %get-tuple-element.232) | copy-start | bytes 17547268
  745.3 74.6 %copy-start.135 = (f32[64,119]{1,0:T(8,128)}, f32[64,119]{1,0:T(8,128)S(1)}, u32[]{:S(2)}) copy-start(f32[64,119]{1,0:T(8,128)S(1)} %broadcast_multiply_fusion.7) | copy-start | bytes 91396
  746.6 73.3 %copy-start.146 = (f32[64,119]{1,0:T(8,128)}, f32[64,119]{1,0:T(8,128)S(1)}, u32[]{:S(2)}) copy-start(f32[64,119]{1,0:T(8,128)S(1)} %add_rsqrt_fusion.1) | copy-start | bytes 91396
  756.8 20.7 copy-start.39
  773.3 33.9 %copy-start.144 = (f32[64,119]{1,0:T(8,128)}, f32[64,119]{1,0:T(8,128)S(1)}, u32[]{:S(2)}) copy-start(f32[64,119]{1,0:T(8,128)S(1)} %broadcast_multiply_fusion.6) | copy-start | bytes 91396
  777.5 29.7 %copy-start.159 = (f32[64,119]{1,0:T(8,128)}, f32[64,119]{1,0:T(8,128)S(1)}, u32[]{:S(2)}) copy-start(f32[64,119]{1,0:T(8,128)S(1)} %add_rsqrt_fusion) | copy-start | bytes 91396
  784.4 22.8 copy-start.175
  784.4 22.8 copy-start.177
  841.6 843.5 %all-gather.36.cloned.1.call-start = ((), (), s32[]{:S(2)}) async-start(), calls=%async_computation.10 | async-start | bytes 5013504 | tf_op jit(solution)/shard_map/all_gather | solution.py:222
  845.9 845.3 %all-gather.38.cloned.1.call-start = ((), (), s32[]{:S(2)}) async-start(), calls=%async_computation.11 | async-start | bytes 5013504 | tf_op jit(solution)/shard_map/all_gather | solution.py:223
  850.4 852.7 %all-gather.32.cloned.1.call-start = ((), (), s32[]{:S(2)}) async-start(), calls=%async_computation.8 | async-start | bytes 5013504 | tf_op jit(solution)/shard_map/all_gather | solution.py:222
  854.8 854.6 %all-gather.34.cloned.1.call-start = ((), (), s32[]{:S(2)}) async-start(), calls=%async_computation.9 | async-start | bytes 5013504 | tf_op jit(solution)/shard_map/all_gather | solution.py:223
  859.1 862.1 %all-gather.28.cloned.1.call-start = ((), (), s32[]{:S(2)}) async-start(), calls=%async_computation.6 | async-start | bytes 5013504 | tf_op jit(solution)/shard_map/all_gather | solution.py:222
  863.5 863.9 %all-gather.30.cloned.1.call-start = ((), (), s32[]{:S(2)}) async-start(), calls=%async_computation.7 | async-start | bytes 5013504 | tf_op jit(solution)/shard_map/all_gather | solution.py:223
  867.8 871.5 %all-gather.24.cloned.1.call-start = ((), (), s32[]{:S(2)}) async-start(), calls=%async_computation.4 | async-start | bytes 5013504 | tf_op jit(solution)/shard_map/all_gather | solution.py:222
  872.2 873.4 %all-gather.26.cloned.1.call-start = ((), (), s32[]{:S(2)}) async-start(), calls=%async_computation.5 | async-start | bytes 5013504 | tf_op jit(solution)/shard_map/all_gather | solution.py:223
  876.6 895.3 %all-gather.20.cloned.1.call-start = ((), (), s32[]{:S(2)}) async-start(), calls=%async_computation.2 | async-start | bytes 5013504 | tf_op jit(solution)/shard_map/all_gather | solution.py:222
  881.0 967.9 %all-gather.22.cloned.1.call-start = ((), (), s32[]{:S(2)}) async-start(), calls=%async_computation.3 | async-start | bytes 5013504 | tf_op jit(solution)/shard_map/all_gather | solution.py:223
  885.3 1041.1 %all-gather.16.cloned.1.call-start = ((), (), s32[]{:S(2)}) async-start(), calls=%async_computation | async-start | bytes 5013504 | tf_op jit(solution)/shard_map/all_gather | solution.py:222
  889.7 1113.7 %all-gather.18.cloned.1.call-start = ((), (), s32[]{:S(2)}) async-start(), calls=%async_computation.1 | async-start | bytes 5013504 | tf_op jit(solution)/shard_map/all_gather | solution.py:223
  894.1 1456.1 %all-reduce.4.cloned.1.call-start = ((), (), s32[]{:S(2)}) async-start(), calls=%async_computation.14 | async-start | bytes 5505024 | tf_op jit(solution)/shard_map/psum | solution.py:339
  894.2 12.2 copy-start.127
  894.2 13.7 copy-start.125
  894.2 13.7 copy-start.153
  894.2 14.4 copy-start.123
  894.2 14.3 copy-start.151
  894.2 15.0 copy-start.121
  894.2 15.0 copy-start.149
  894.2 15.6 copy-start.40
  894.2 15.6 copy-start.145
  894.2 15.6 copy-start.160
  894.3 15.6 copy-start.176
  894.3 15.6 copy-start.178
  898.2 27.5 %slice-start.2 = ((s8[6291456]{0:T(1024)(128)(4,1)}), s8[4194304]{0:T(1024)(128)(4,1)S(1)}, s32[]{:S(2)}) async-start(s8[6291456]{0:T(1024)(128)(4,1)} %bitcast.489), calls=%async_computation.17 | async-start | bytes 8388608
  909.9 15.7 slice-start.3
  909.9 15.7 copy-start.14
  925.7 13.9 copy-start.97
  925.7 14.7 copy-start.96
  1203.5 46.9 %copy-start.119 = (f32[17,6,64]{2,1,0:T(8,128)S(1)}, f32[17,6,64]{2,1,0:T(8,128)}, u32[]{:S(2)}) copy-start(f32[17,6,64]{2,1,0:T(8,128)} %get-tuple-element.168) | copy-start | bytes 78340
  1318.1 38.2 %copy-start.134 = (bf16[17,6,64]{0,1,2:T(8,128)(2,1)S(1)}, bf16[17,6,64]{0,1,2:T(8,128)(2,1)}, u32[]{:S(2)}) copy-start(bf16[17,6,64]{0,1,2:T(8,128)(2,1)} %copy.1012) | copy-start | bytes 39172
  1319.5 74.3 %copy-start.133 = (bf16[17,6,64]{0,1,2:T(8,128)(2,1)S(1)}, bf16[17,6,64]{0,1,2:T(8,128)(2,1)}, u32[]{:S(2)}) copy-start(bf16[17,6,64]{0,1,2:T(8,128)(2,1)} %copy.1001) | copy-start | bytes 39172
  1355.6 74.3 %copy-start.132 = (bf16[17,6,64]{0,1,2:T(8,128)(2,1)S(1)}, bf16[17,6,64]{0,1,2:T(8,128)(2,1)}, u32[]{:S(2)}) copy-start(bf16[17,6,64]{0,1,2:T(8,128)(2,1)} %copy.990) | copy-start | bytes 39172
  1393.1 72.8 %copy-start.131 = (bf16[17,6,64]{0,1,2:T(8,128)(2,1)S(1)}, bf16[17,6,64]{0,1,2:T(8,128)(2,1)}, u32[]{:S(2)}) copy-start(bf16[17,6,64]{0,1,2:T(8,128)(2,1)} %copy.979) | copy-start | bytes 39172
  1612.2 44.7 %copy-start.41 = (bf16[1,64,119,192]{2,3,1,0:T(8,128)(2,1)S(1)}, bf16[1,64,119,192]{2,3,1,0:T(8,128)(2,1)}, u32[]{:S(2)}) copy-start(bf16[1,64,119,192]{2,3,1,0:T(8,128)(2,1)} %param.16) | copy-start | bytes 8773636
  1617.2 41.0 %copy-start.136 = (f32[64,119]{1,0:T(8,128)S(1)}, f32[64,119]{1,0:T(8,128)}, u32[]{:S(2)}) copy-start(f32[64,119]{1,0:T(8,128)} %copy-done.135) | copy-start | bytes 91396
  1617.2 41.0 %copy-start.147 = (f32[64,119]{1,0:T(8,128)S(1)}, f32[64,119]{1,0:T(8,128)}, u32[]{:S(2)}) copy-start(f32[64,119]{1,0:T(8,128)} %copy-done.146) | copy-start | bytes 91396
  1617.2 41.0 %copy-start.186 = (f32[1,192]{1,0:T(1,128)S(1)}, f32[1,192]{1,0:T(1,128)}, u32[]{:S(2)}) copy-start(f32[1,192]{1,0:T(1,128)} %get-tuple-element.202) | copy-start | bytes 2308
  1778.1 76.9 %copy-start.162 = (bf16[4,17,6,32]{3,0,2,1:T(4,128)(2,1)S(1)}, bf16[4,17,6,32]{3,0,2,1:T(4,128)(2,1)}, u32[]{:S(2)}) copy-start(bf16[4,17,6,32]{3,0,2,1:T(4,128)(2,1)} %copy.962) | copy-start | bytes 78340
  1860.7 72.0 %copy-start.161 = (bf16[4,17,6,32]{3,0,2,1:T(4,128)(2,1)S(1)}, bf16[4,17,6,32]{3,0,2,1:T(4,128)(2,1)}, u32[]{:S(2)}) copy-start(bf16[4,17,6,32]{3,0,2,1:T(4,128)(2,1)} %copy.951) | copy-start | bytes 78340
  2052.4 19.8 slice-start.4
  2080.3 12.3 copy-start.89
  2109.5 20.5 copy-start.44
  2195.6 15.8 copy-start.168
  2352.4 24.6 %copy-start.36 = (f32[6,192,192]{1,2,0:T(8,128)S(1)}, f32[6,192,192]{1,2,0:T(8,128)}, u32[]{:S(2)}) copy-start(f32[6,192,192]{1,2,0:T(8,128)} %get-tuple-element.137) | copy-start | bytes 2654212
  2352.4 25.1 %copy-start.47 = (f32[6,192,192]{1,2,0:T(8,128)S(1)}, f32[6,192,192]{1,2,0:T(8,128)}, u32[]{:S(2)}) copy-start(f32[6,192,192]{1,2,0:T(8,128)} %copy.867) | copy-start | bytes 2654212
  (157 other events, 661.5 us)
Sparse Core Ops, SparseCore 0:
  77.4 89.6 all-gather.39
  841.7 85.3 all-gather.41
  929.3 105.4 all-gather.35
  1036.8 105.6 all-gather.37
  1144.5 101.9 all-gather.31
  1248.6 96.1 all-gather.33
  1347.0 93.5 all-gather.27
  1442.8 93.0 all-gather.29
  1538.1 76.3 all-gather.23
  1616.5 78.2 all-gather.25
  1697.1 74.8 all-gather.19
  1774.0 74.8 all-gather.21
  1851.6 74.8 all-gather.15
  1928.5 74.8 all-gather.17
  2211.5 138.6 all-reduce.3
where the time goes:
time: 2410 us; the launch traced here: 2400 us
  blocking collectives  1040 us (43%)
  local copies, waits for them, and re-layouts  538 us (22%)
  waiting for transfers between devices  345 us (14%)
  matrix products  329 us (14%)
  other arithmetic  124 us (5%)
    all_gather x7, blocking collectives, on_device(): lax.all_gather(lse_block.astype(jnp.bfloat16), 'rows', axis=2, tiled=True)  262 us
    all_gather x7, blocking collectives, on_device(): lax.all_gather(offset.astype(jnp.bfloat16), 'rows', axis=2, tiled=True)  247 us
    all_gather x7, blocking collectives, on_device(): lax.all_gather(key_item[:, columns], 'rows', axis=0, tiled=True)  234 us
    all_gather x7, blocking collectives, on_device(): lax.all_gather(value_item[:, columns], 'rows', axis=0, tiled=True)  232 us
    all_gather x7, waiting for transfers between devices, on_device(): lax.all_gather(grad_block, 'rows', axis=0, tiled=True)  138 us
    psum x1, waiting for transfers between devices, on_device(): lax.psum((proj_grad, out_grad, in_grad, hid_grad, norm_grad), ('table', '...  127 us
    reshape x35, local copies, waits for them, and re-layouts, split_heads(): return value.reshape(value.shape[:-1] + (HEADS, HEAD))  119 us
    dot_general x20, matrix products, product(): return jnp.dot(left, right, preferred_element_type=jnp.float32)  114 us
  transfers between devices with their start and end apart: 15, of which 5 were waited for; matrix products, arithmetic and copies ran while one was open for 29% of the time, Pallas kernels for 0%

commit v1 on v0

v1 whole, which is shorter than its diff:
```python
import functools

import jax
import jax.numpy as jnp
import numpy as np
from jax import lax
from jax.experimental import pallas as pl
from jax.experimental.pallas import tpu as pltpu
from jax.sharding import PartitionSpec as P

BF, F32 = jnp.bfloat16, jnp.float32
D, DP = 192, 256
H, E = 6, 32
F, FP = 119, 128
FS = 120
FF = 768
STEP = 3
CLIP = 0.3
RATE = 0.5
SCALE = E**-0.5
SCALE2 = SCALE * 1.4426950408889634
C0 = 0.7978845608028654
C1 = 0.044715
NT = (((1,), (1,)), ((), ()))
TN = (((0,), (0,)), ((), ()))
PAIR = 576
TAIL = 3 * PAIR + 8
MID = 2 * 6 * D + PAIR + 8


def mm(a, b):
    return jnp.dot(a, b, preferred_element_type=F32)


def mm_nt(a, b):
    return lax.dot_general(a, b, NT, preferred_element_type=F32)


def mm_tn(a, b):
    return lax.dot_general(a, b, TN, preferred_element_type=F32)


def lanes():
    return lax.broadcasted_iota(jnp.int32, (1, DP), 1)


def head_masks():
    lane = lanes()
    return [
        jnp.where((lane >= E * h) & (lane < E * (h + 1)), 1.0, 0.0).astype(BF) for h in range(H)
    ]


def spread(w, masks):
    return jnp.concatenate([w * m for m in masks], 0)


def layer_norm(a, lane_ok):
    c = a - jnp.sum(a, -1, keepdims=True) * (1.0 / D) * lane_ok
    rc = lax.rsqrt(jnp.sum(c * c, -1, keepdims=True) * (1.0 / D) + 1e-5)
    return c * rc, rc


def norm_back(g, n, rc, gain, lane_ok):
    dn = g * gain
    m1 = jnp.sum(dn, -1, keepdims=True) * (1.0 / D)
    m2 = jnp.sum(dn * n, -1, keepdims=True) * (1.0 / D)
    return (dn - m1 * lane_ok - n * m2) * rc


def fold8(v):
    return jnp.sum(v.reshape(v.shape[0] // 8, 8, v.shape[1]), 0)


def diagonal(full, keys):
    lane = lax.broadcasted_iota(jnp.int32, (1, 128), 1)
    low = full[0:keys, 0:128]
    for h in range(1, 4):
        low = jnp.where(lane >= E * h, full[h * keys : (h + 1) * keys, 0:128], low)
    high = jnp.where(
        lane >= E, full[5 * keys : 6 * keys, 128:256], full[4 * keys : 5 * keys, 128:256]
    )
    return jnp.concatenate([low, high], 1)


def whole(a):
    nd = len(a.shape)
    return pl.BlockSpec(a.shape, lambda *i: (0,) * nd)


def shape(s, t=BF):
    return jax.ShapeDtypeStruct(s, t)


def params(mib=58):
    return pltpu.CompilerParams(vmem_limit_bytes=mib << 20)


def perm_matrix():
    place = np.zeros((256, 256), np.float32)
    for f in range(16):
        for r in range(16):
            place[f * 16 + r, r * 16 + f] = 1
    return jnp.asarray(place, BF)


def prep_kernel(
    proj, outw, w_in, w_out, norms, wqkv, wqkvT, wo, woT, wkv2, wk2T, wv2T, wq2, wq2T, wo2, wo2T, w1, w1T, w2, w2T, np8
):
    zc = jnp.zeros((D, DP - D), F32)
    zr = jnp.zeros((DP - D, DP), BF)

    def square(w):
        a = jnp.concatenate([w, zc], 1)
        a = jnp.concatenate([a.astype(BF), zr], 0)
        return a, a.T

    for i in range(3):
        a, t = square(proj[i])
        wqkv[:, i * DP : (i + 1) * DP] = a
        wqkvT[i * DP : (i + 1) * DP, :] = t
    for src, dst, dstT in ((outw[0], wo, woT), (proj[3], wq2, wq2T), (outw[1], wo2, wo2T)):
        a, t = square(src)
        dst[...] = a
        dstT[...] = t
    a, t = square(proj[4])
    wk2T[...] = t
    a, t = square(proj[5])
    wv2T[...] = t
    wkv2[0:D, :] = jnp.concatenate([proj[4], proj[5]], 1).astype(BF)
    wkv2[D:DP, :] = jnp.zeros((DP - D, 2 * D), BF)
    a = jnp.concatenate([w_in[...].astype(BF), jnp.zeros((DP - D, FF), BF)], 0)
    w1[...] = a
    w1T[...] = a.T
    a = jnp.concatenate([w_out[...], jnp.zeros((FF, DP - D), F32)], 1).astype(BF)
    w2[...] = a
    w2T[...] = a.T
    np8[...] = jnp.zeros((8, DP), F32)
    np8[0:6, 0:D] = norms[...]


def prepare(proj, outw, w_in, w_out, norms):
    sq = shape((DP, DP))
    outs = [
        shape((DP, 3 * DP)),
        shape((3 * DP, DP)),
        sq,
        sq,
        shape((DP, 2 * D)),
        sq,
        sq,
        sq,
        sq,
        sq,
        sq,
        shape((DP, FF)),
        shape((FF, DP)),
        shape((FF, DP)),
        shape((DP, FF)),
        shape((8, DP), F32),
    ]
    return pl.pallas_call(prep_kernel, out_shape=outs, compiler_params=params(), name="weights")(
        proj, outw, w_in, w_out, norms
    )


def feature_rows(x, wqkv, wo, masks, lane_ok, U, keep=None):
    qkv = mm(x, wqkv).astype(BF)
    outs = []
    for u in range(U):
        own = qkv[u * FP : (u + 1) * FP]
        q, k, v = own[:, 0:DP], own[:, DP : 2 * DP], own[:, 2 * DP : 3 * DP]
        st = mm_nt(k, spread(q, masks))
        row = lax.broadcasted_iota(jnp.int32, (8, 1), 0)
        st = jnp.concatenate([st[: FS - 8], jnp.where(row < F - FS + 8, st[FS - 8 : FS], -1e30)], 0)
        mx = jnp.max(st, 0, keepdims=True)
        e = jnp.exp2((st - mx) * SCALE2)
        total = jnp.sum(e, 0, keepdims=True)
        p = e * (1.0 / total)
        p = jnp.concatenate([p, jnp.zeros((FP - FS, H * FP), F32)], 0).astype(BF)
        vt = v.T
        ot = []
        for j in range(H // 2):
            t = mm(vt[64 * j : 64 * j + 64], p[:, 256 * j : 256 * j + 256])
            ot += [t[0:32, 0:128], t[32:64, 128:256]]
        ot = jnp.concatenate(ot + [jnp.zeros((DP - D, FP), F32)], 0).astype(BF)
        o = ot.T
        if keep is not None:
            keep(u, own, p, o)
        outs.append(o)
    o = jnp.concatenate(outs, 0)
    return layer_norm(x.astype(F32) + mm(o, wo), lane_ok)


def slots_kernel(SL, count_ref, mask_ref, order_ref, x_ref, wqkv_ref, wo_ref, wkv2_ref, np_ref, kv_ref, xs):
    xs[...] = jnp.zeros_like(xs)
    masks = head_masks()
    lane_ok = (lanes() < D).astype(F32)
    for u in range(SL):
        xs[u * FP : u * FP + F, 0:D] = x_ref[u]
    n, _ = feature_rows(xs[...], wqkv_ref[...], wo_ref[...], masks, lane_ok, SL)
    h = (n * np_ref[0:1, :] + np_ref[1:2, :]).astype(BF)
    kv = mm(h, wkv2_ref[...])
    row = lax.broadcasted_iota(jnp.int32, (FS, 1), 0)
    for u in range(SL):
        order = order_ref[0, u]
        usable = (order < count_ref[0]) & ((mask_ref[0, u] == 1) | (order == 0))
        flag = jnp.where(usable, 1.0, 0.0)
        kv_ref[u] = jnp.where(row < F, kv[u * FP : u * FP + FS], flag).astype(BF)


def slot_keys(count, mask, order, cells, wqkv, wo, wkv2, np8):
    SL = mask.shape[1]
    smem = pl.BlockSpec(memory_space=pltpu.SMEM)
    return pl.pallas_call(
        functools.partial(slots_kernel, SL),
        grid=(1,),
        in_specs=[smem, smem, smem, pl.BlockSpec((SL, F, D), lambda i: (0, 0, 0))]
        + [whole(a) for a in (wqkv, wo, wkv2, np8)],
        out_specs=pl.BlockSpec((SL, FS, 2 * D), lambda i: (0, 0, 0)),
        out_shape=shape((SL, FS, 2 * D)),
        scratch_shapes=[pltpu.VMEM((SL * FP, DP), BF)],
        compiler_params=params(),
        name="slot_keys",
    )(count, mask, order, cells, wqkv, wo, wkv2, np8)


def forward_kernel(R, U, x_ref, wqkv_ref, wo_ref, perm_ref, nt_ref, n_ref, qkv_ref, p_ref, of_ref, xs):
    @pl.when(pl.program_id(0) == 0)
    def _():
        xs[...] = jnp.zeros_like(xs)

    masks = head_masks()
    lane = lanes()
    lane_ok = (lane < D).astype(F32)

    def rows(i, carry):
        r0 = i * U
        for u in range(U):
            xs[u * FP : u * FP + F, 0:D] = x_ref[r0 + u]

        def keep(u, own, p, o):
            qkv_ref[r0 + u] = own
            p_ref[r0 + u] = p
            of_ref[r0 + u] = o

        n, rc = feature_rows(xs[...], wqkv_ref[...], wo_ref[...], masks, lane_ok, U, keep)
        n = jnp.where(lane >= D, rc, n).astype(BF)
        for u in range(U):
            n_ref[r0 + u] = n[u * FP : (u + 1) * FP]
        return carry

    lax.fori_loop(0, R // U, rows, 0)

    def turn(j, carry):
        f0 = pl.multiple_of(j * 16, 16)
        block = n_ref[:, pl.ds(f0, 16), :].reshape(R * 16, DP)
        nt_ref[pl.ds(f0, 16)] = mm(perm_ref[...], block).astype(BF).reshape(16, R, DP)
        return carry

    lax.fori_loop(0, FP // 16, turn, 0)


def feature_forward(cells, wqkv, wo, perm, R=16, U=4):
    rows = cells.shape[0]
    nat = lambda w: pl.BlockSpec((R, FP, w), lambda i: (i, 0, 0))
    return pl.pallas_call(
        functools.partial(forward_kernel, R, U),
        grid=(rows // R,),
        in_specs=[pl.BlockSpec((R, F, D), lambda i: (i, 0, 0)), whole(wqkv), whole(wo), whole(perm)],
        out_specs=[
            pl.BlockSpec((FP, R, DP), lambda i: (0, i, 0)),
            nat(DP),
            nat(3 * DP),
            nat(H * FP),
            nat(DP),
        ],
        out_shape=[
            shape((FP, rows, DP)),
            shape((rows, FP, DP)),
            shape((rows, FP, 3 * DP)),
            shape((rows, FP, H * FP)),
            shape((rows, FP, DP)),
        ],
        scratch_shapes=[pltpu.VMEM((U * FP, DP), BF)],
        compiler_params=params(),
        name="feature_forward",
    )(cells, wqkv, wo, perm)


def columns_kernel(x_ref, perm_ref, out_ref, xs):
    xs[...] = jnp.zeros_like(xs)
    xs[:, 0:F, 0:D] = x_ref[...]

    def turn(j, carry):
        f0 = pl.multiple_of(j * 16, 16)
        block = xs[:, pl.ds(f0, 16), :].reshape(256, DP)
        out_ref[pl.ds(f0, 16)] = mm(perm_ref[...], block).astype(BF).reshape(16, 16, DP)
        return carry

    lax.fori_loop(0, FP // 16, turn, 0)


def to_columns(x, perm):
    rows = x.shape[0]
    return pl.pallas_call(
        columns_kernel,
        grid=(rows // 16,),
        in_specs=[pl.BlockSpec((16, F, D), lambda i: (i, 0, 0)), whole(perm)],
        out_specs=pl.BlockSpec((FP, 16, DP), lambda i: (0, i, 0)),
        out_shape=shape((FP, rows, DP)),
        scratch_shapes=[pltpu.VMEM((16, FP, DP), BF)],
        compiler_params=params(),
        name="to_columns",
    )(x, perm)


def gathered_kernel(kv_ref, perm_ref, kt_ref, vt_ref, bias_ref, xs):
    xs[:, FS:FP, :] = jnp.zeros((16, FP - FS, 2 * D), BF)
    xs[:, 0:FS, :] = kv_ref[...]
    kt_ref[:, :, D:DP] = jnp.zeros((FP, 16, DP - D), BF)
    vt_ref[:, :, D:DP] = jnp.zeros((FP, 16, DP - D), BF)
    for j in range(FP // 16):
        f0 = 16 * j
        block = mm(perm_ref[...], xs[:, f0 : f0 + 16, :].reshape(256, 2 * D))
        if f0 < F <= f0 + 16:
            flag = block[(F - f0) * 16 : (F - f0 + 1) * 16, 0:128]
            bias_ref[...] = jnp.where(flag > 0.5, 0.0, -1e30)
        kt_ref[f0 : f0 + 16, :, 0:D] = block[:, 0:D].astype(BF).reshape(16, 16, D)
        vt_ref[f0 : f0 + 16, :, 0:D] = block[:, D : 2 * D].astype(BF).reshape(16, 16, D)


def gathered_columns(kv, perm):
    keys = kv.shape[0]
    col = pl.BlockSpec((FP, 16, DP), lambda i: (0, i, 0))
    return pl.pallas_call(
        gathered_kernel,
        grid=(keys // 16,),
        in_specs=[pl.BlockSpec((16, FS, 2 * D), lambda i: (i, 0, 0)), whole(perm)],
        out_specs=[col, col, pl.BlockSpec((16, 128), lambda i: (i, 0))],
        out_shape=[shape((FP, keys, DP)), shape((FP, keys, DP)), shape((keys, 128), F32)],
        scratch_shapes=[pltpu.VMEM((16, FP, 2 * D), BF)],
        compiler_params=params(),
        name="gathered_columns",
    )(kv, perm)


def parts_kernel(dk_ref, dv_ref, perm_ref, out_ref):
    col = lax.broadcasted_iota(jnp.int32, (16, 1, 1), 0)
    for j in range(FP // 16):
        f0 = 16 * j
        n = min(16, FS - f0)
        turned = []
        for ref in (dk_ref, dv_ref):
            block = ref[f0 : f0 + 16]
            if f0 + 16 > F:
                block = jnp.where(col < F - f0, block, 0).astype(BF)
            turned.append(mm(perm_ref[...], block.reshape(256, DP))[:, 0:D])
        both = jnp.concatenate(turned, 1).astype(BF).reshape(16, 16, 2 * D)
        out_ref[:, f0 : f0 + n, :] = both[:, 0:n, :]


def slot_parts(dk, dv, perm):
    keys = dk.shape[1]
    col = pl.BlockSpec((FP, 16, DP), lambda i: (0, i, 0))
    return pl.pallas_call(
        parts_kernel,
        grid=(keys // 16,),
        in_specs=[col, col, whole(perm)],
        out_specs=pl.BlockSpec((16, FS, 2 * D), lambda i: (i, 0, 0)),
        out_shape=shape((keys, FS, 2 * D)),
        compiler_params=params(),
        name="slot_parts",
    )(dk, dv, perm)


def pack_pair(ref, at, a, b):
    ref[at : at + D] = a[0:D, 0:128].astype(BF)
    ref[at + D : at + 2 * D] = b[0:D, 0:128].astype(BF)
    ref[at + 2 * D : at + 3 * D] = jnp.concatenate([a[0:D, 128:D], b[0:D, 128:D]], 1).astype(BF)


def pack_norms(ref, at, sums):
    rows = []
    for s in sums:
        v = jnp.sum(s, 0, keepdims=True)
        rows += [v[:, 0:128], v[:, 128:256]]
    rows.append(jnp.zeros((ref.shape[0] - at - len(rows), 128), F32))
    ref[at:] = jnp.concatenate(rows, 0).astype(BF)


def item_kernel(
    FB, RW, keys, CH, nt_ref, ct_ref, kt_ref, vt_ref, bias_ref, wq_ref, wqT_ref, wo_ref, woT_ref, w1_ref, w1T_ref,
    w2_ref, w2T_ref, np_ref, y_ref, g1_ref, dk_ref, dv_ref, pack_ref, dwq, dwo, dw1, dw2, dnp, h1b, qs, pbs, oi, da2s,
    dab, doi, dqs, h2b, dub, dbr, acts,
):
    M = FB * RW

    @pl.when(pl.program_id(0) == 0)
    def _():
        for ref in (dwq, dwo, dw1, dw2, dnp):
            ref[...] = jnp.zeros_like(ref)

    masks = head_masks()
    lane_ok = (lanes() < D).astype(F32)
    g0, b0, g1, b1, g2, b2 = [np_ref[i : i + 1, :] for i in range(6)]
    left = lax.broadcasted_iota(jnp.int32, (1, 2 * RW), 1) < RW
    HK = H * keys

    def attend(j, carry):
        s0 = pl.multiple_of(j * 2 * RW, 2 * RW)
        n = nt_ref[pl.ds(2 * j, 2)].reshape(2 * RW, DP).astype(F32)
        hb = (n * g0 + b0).astype(BF)
        h1b[pl.ds(s0, 2 * RW)] = hb
        q = mm(hb, wq_ref[...]).astype(BF)
        qs[pl.ds(s0, 2 * RW)] = q
        ka, kb = spread(kt_ref[2 * j], masks), spread(kt_ref[2 * j + 1], masks)
        st = jnp.where(left, mm_nt(ka, q), mm_nt(kb, q))
        st = st.reshape(H, keys, 2 * RW) + bias_ref[...][None]
        mx = jnp.max(st, 1, keepdims=True)
        e = jnp.exp2((st - mx) * SCALE2)
        total = jnp.sum(e, 1, keepdims=True)
        pb = (e * (1.0 / total)).reshape(HK, 2 * RW).astype(BF)
        pbs[j] = pb
        pt = pb.T
        va, vb = spread(vt_ref[2 * j], masks), spread(vt_ref[2 * j + 1], masks)
        oi[pl.ds(s0, RW)] = mm(pt[:RW], va).astype(BF)
        oi[pl.ds(s0 + RW, RW)] = mm(pt[RW:], vb).astype(BF)
        return carry

    lax.fori_loop(0, FB // 2, attend, 0)

    def dense(j, carry):
        gs2, bs2, gs1, bs1 = carry
        s0 = pl.multiple_of(j * CH, CH)
        cols = CH // RW
        h1 = nt_ref[pl.ds(j * cols, cols)].reshape(CH, DP).astype(F32) * g0 + b0
        n2, rc2 = layer_norm(h1 + mm(oi[pl.ds(s0, CH)], wo_ref[...]), lane_ok)
        h2 = n2 * g1 + b1
        hb = h2.astype(BF)
        h2b[pl.ds(s0, CH)] = hb
        u = mm(hb, w1_ref[...])
        uu = u * u
        th = jnp.tanh(u * (C0 + (C0 * C1) * uu))
        half = 0.5 + 0.5 * th
        act = (u * half).astype(BF)
        acts[pl.ds(s0, CH)] = act
        slope = half + (0.5 * u) * (1.0 - th * th) * (C0 + (3.0 * C0 * C1) * uu)
        n3, rc3 = layer_norm(h2 + mm(act, w2_ref[...]), lane_ok)
        y_ref[pl.ds(j * cols, cols)] = (n3 * g2 + b2).astype(BF).reshape(cols, RW, DP)
        g = ct_ref[pl.ds(j * cols, cols)].reshape(CH, DP).astype(F32)
        gs2 = gs2 + fold8(g * n3)
        bs2 = bs2 + fold8(g)
        d3 = norm_back(g, n3, rc3, g2, lane_ok)
        db = d3.astype(BF)
        dbr[pl.ds(s0, CH)] = db
        du = (mm(db, w2T_ref[...]) * slope).astype(BF)
        dub[pl.ds(s0, CH)] = du
        dh2 = d3 + mm(du, w1T_ref[...])
        gs1 = gs1 + fold8(dh2 * n2)
        bs1 = bs1 + fold8(dh2)
        d2 = norm_back(dh2, n2, rc2, g1, lane_ok)
        da2s[pl.ds(s0, CH)] = d2
        d2b = d2.astype(BF)
        dab[pl.ds(s0, CH)] = d2b
        doi[pl.ds(s0, CH)] = mm(d2b, woT_ref[...]).astype(BF)
        return gs2, bs2, gs1, bs1

    z = jnp.zeros((8, DP), F32)
    gs2, bs2, gs1, bs1 = lax.fori_loop(0, M // CH, dense, (z, z, z, z))
    dnp[0] += gs1
    dnp[1] += bs1
    dnp[2] += gs2
    dnp[3] += bs2
    zero = jnp.zeros((RW, DP), BF)

    def back(j, carry):
        s0 = pl.multiple_of(j * 2 * RW, 2 * RW)
        q, do = qs[pl.ds(s0, 2 * RW)], doi[pl.ds(s0, 2 * RW)]
        pb = pbs[j]
        ka, kb = spread(kt_ref[2 * j], masks), spread(kt_ref[2 * j + 1], masks)
        va, vb = spread(vt_ref[2 * j], masks), spread(vt_ref[2 * j + 1], masks)
        dp = jnp.where(left, mm_nt(va, do), mm_nt(vb, do)).reshape(H, keys, 2 * RW)
        p = pb.astype(F32).reshape(H, keys, 2 * RW)
        off = jnp.sum(p * dp, 1, keepdims=True)
        ds = (p * (dp - off)).reshape(HK, 2 * RW).astype(BF)
        dst = ds.T
        dq = jnp.concatenate([mm(dst[:RW], ka), mm(dst[RW:], kb)], 0) * SCALE
        dqs[pl.ds(s0, 2 * RW)] = dq.astype(BF)
        for c in range(2):
            part = slice(c * RW, (c + 1) * RW)
            qz = jnp.concatenate([q[part], zero] if c == 0 else [zero, q[part]], 0)
            dz = jnp.concatenate([do[part], zero] if c == 0 else [zero, do[part]], 0)
            dk_ref[2 * j + c] = (diagonal(mm(ds, qz), keys) * SCALE).astype(BF)
            dv_ref[2 * j + c] = diagonal(mm(pb, dz), keys).astype(BF)
        return carry

    lax.fori_loop(0, FB // 2, back, 0)

    def finish(j, carry):
        s0 = pl.multiple_of(j * CH, CH)
        cols = CH // RW
        g = da2s[pl.ds(s0, CH)] + mm(dqs[pl.ds(s0, CH)], wqT_ref[...])
        g1_ref[pl.ds(j * cols, cols)] = g.astype(BF).reshape(cols, RW, DP)
        return carry

    lax.fori_loop(0, M // CH, finish, 0)
    dwq[...] += mm_tn(h1b[...], dqs[...])
    dwo[...] += mm_tn(oi[...], dab[...])
    dw1[...] += mm_tn(h2b[...], dub[...])
    dw2[...] += mm_tn(dbr[...], acts[...])

    @pl.when(pl.program_id(0) == pl.num_programs(0) - 1)
    def _():
        at = 0
        for ref in (dw1, dw2):
            for j in range(FF // 128):
                pack_ref[at : at + D] = ref[0:D, 128 * j : 128 * j + 128].astype(BF)
                at += D
        pack_pair(pack_ref, at, dwq, dwo)
        pack_norms(pack_ref, at + PAIR, [dnp[i] for i in range(4)])


def item_and_dense(nt, ct, kt, vt, bias, ws, np8, packed, FB=8, CH=128):
    RW = nt.shape[1]
    keys = kt.shape[1]
    M = FB * RW
    cells = pl.BlockSpec((FB, RW, DP), lambda i: (i, 0, 0))
    slots = pl.BlockSpec((FB, keys, DP), lambda i: (i, 0, 0))
    own = pltpu.VMEM((M, DP), BF)
    wide = pltpu.VMEM((M, FF), BF)
    return pl.pallas_call(
        functools.partial(item_kernel, FB, RW, keys, CH),
        grid=(pl.cdiv(F, FB),),
        in_specs=[cells, cells, slots, slots, whole(bias)] + [whole(w) for w in ws] + [whole(np8)],
        out_specs=[cells, cells, slots, slots, pl.BlockSpec((packed, 128), lambda i: (0, 0))],
        out_shape=[shape((FP, RW, DP))] * 2 + [shape((FP, keys, DP))] * 2 + [shape((packed, 128))],
        scratch_shapes=[
            pltpu.VMEM((DP, DP), F32),
            pltpu.VMEM((DP, DP), F32),
            pltpu.VMEM((DP, FF), F32),
            pltpu.VMEM((DP, FF), F32),
            pltpu.VMEM((4, 8, DP), F32),
            own,
            own,
            pltpu.VMEM((FB // 2, H * keys, 2 * RW), BF),
            own,
            pltpu.VMEM((M, DP), F32),
            own,
            own,
            own,
            own,
            wide,
            own,
            wide,
        ],
        compiler_params=params(),
        name="item_and_dense",
    )(nt, ct, kt, vt, bias, *ws, np8)


def backward_kernel(R, U, SL, x_ref, qkv_ref, p_ref, of_ref, n_ref, g1t_ref, yt_ref, *rest):
    if SL:
        (dkv_ref, wk2T_ref, wv2T_ref, wqkvT_ref, woT_ref, np_ref, perm_ref, iqkv, iwo, inp, _, _,
         cg_ref, y_ref, pack_ref, gs, xs, dqkvs, dfbs, dqkv, dwo, dnp) = rest
    else:
        wqkvT_ref, woT_ref, np_ref, perm_ref, cg_ref, y_ref, dqkv, dwo, dnp, gs, xs, dqkvs, dfbs = rest
    masks = head_masks()
    lane_ok = (lanes() < D).astype(F32)

    @pl.when(pl.program_id(0) == 0)
    def _():
        xs[...] = jnp.zeros_like(xs)
        for i, ref in enumerate((dqkv, dwo, dnp)):
            ref[...] = (iqkv, iwo, inp)[i][...] if SL else jnp.zeros_like(ref)

    g0, b0 = np_ref[0:1, :], np_ref[1:2, :]
    col = lax.broadcasted_iota(jnp.int32, (16, 1, 1), 0)

    def turn(j, carry):
        f0 = pl.multiple_of(j * 16, 16)
        block = jnp.where(col < F - f0, g1t_ref[pl.ds(f0, 16)], 0).astype(BF).reshape(256, DP)
        gs[:, pl.ds(f0, 16)] = mm(perm_ref[...], block).reshape(R, 16, DP)
        return carry

    lax.fori_loop(0, FP // 16, turn, 0)

    def turn_y(j, carry):
        f0 = pl.multiple_of(j * 16, 16)
        block = yt_ref[pl.ds(f0, 16)].reshape(256, DP)
        y_ref[:, pl.ds(f0, 16), :] = mm(perm_ref[...], block).astype(BF).reshape(R, 16, DP)[:, :, 0:D]
        return carry

    lax.fori_loop(0, FP // 16 - 1, turn_y, 0)
    f0 = FP - 16
    block = jnp.where(col < F - f0, yt_ref[f0:FP], 0).astype(BF).reshape(256, DP)
    y_ref[:, f0:F, :] = mm(perm_ref[...], block).astype(BF).reshape(R, 16, DP)[:, 0 : F - f0, 0:D]

    if SL:
        both = dkv_ref[0].astype(F32)
        for i in range(1, dkv_ref.shape[0]):
            both = both + dkv_ref[i].astype(F32)
        both = both.astype(BF)
        z0 = jnp.zeros((SL, FP - FS, 2 * D), BF)
        zc = jnp.zeros((SL * FP, DP - D), BF)
        both = jnp.concatenate([both, z0], 1).reshape(SL * FP, 2 * D)
        dk2 = jnp.concatenate([both[:, 0:D], zc], 1)
        dv2 = jnp.concatenate([both[:, D : 2 * D], zc], 1)
        gs[0:SL] += (mm(dk2, wk2T_ref[...]) + mm(dv2, wv2T_ref[...])).reshape(SL, FP, DP)
        h1 = (n_ref[0:SL].astype(F32).reshape(SL * FP, DP) * g0 + b0).astype(BF)
        pack_pair(pack_ref, 2 * PAIR, mm_tn(h1, dk2), mm_tn(h1, dv2))

    def rows(i, carry):
        gsum, bsum = carry
        r0 = i * U
        g = gs[pl.ds(r0, U)].reshape(U * FP, DP)
        nf = n_ref[pl.ds(r0, U)].reshape(U * FP, DP).astype(F32)
        rc = nf[:, D : D + 1]
        n = nf * lane_ok
        gsum = gsum + fold8(g * n)
        bsum = bsum + fold8(g)
        da = norm_back(g, n, rc, g0, lane_ok)
        dfb = da.astype(BF)
        dfbs[pl.ds(pl.multiple_of(r0 * FP, FP), U * FP)] = dfb
        doa = mm(dfb, woT_ref[...]).astype(BF)
        outs = []
        for u in range(U):
            do = doa[u * FP : (u + 1) * FP]
            q = qkv_ref[r0 + u, :, 0:DP]
            k = qkv_ref[r0 + u, :, DP : 2 * DP]
            v = qkv_ref[r0 + u, :, 2 * DP : 3 * DP]
            p = p_ref[r0 + u]
            dom = spread(do, masks)
            dp = mm_nt(v, dom)
            pf = p.astype(F32)
            off = jnp.sum(pf * dp, 0, keepdims=True)
            ds = (pf * (dp - off)).astype(BF)
            dk = (mm(ds, spread(q, masks)) * SCALE).astype(BF)
            dv = mm(p, dom).astype(BF)
            kt = k.T
            dqt = []
            for j in range(H // 2):
                t = mm(kt[64 * j : 64 * j + 64], ds[:, 256 * j : 256 * j + 256])
                dqt += [t[0:32, 0:128], t[32:64, 128:256]]
            dqt = (jnp.concatenate(dqt + [jnp.zeros((DP - D, FP), F32)], 0) * SCALE).astype(BF)
            outs.append(jnp.concatenate([dqt.T, dk, dv], 1))
        all3 = jnp.concatenate(outs, 0)
        dqkvs[pl.ds(pl.multiple_of(r0 * FP, FP), U * FP)] = all3
        cg = da + mm(all3, wqkvT_ref[...])
        for u in range(U):
            cg_ref[r0 + u] = cg[u * FP : u * FP + F, 0:D]
            xs[r0 + u, 0:F, 0:D] = x_ref[r0 + u]
        return gsum, bsum

    z = jnp.zeros((8, DP), F32)
    gsum, bsum = lax.fori_loop(0, R // U, rows, (z, z))
    dnp[0] += gsum
    dnp[1] += bsum
    dqkv[...] += mm_tn(xs[...].reshape(R * FP, DP), dqkvs[...])
    dwo[...] += mm_tn(of_ref[...].reshape(R * FP, DP), dfbs[...])

    if SL:

        @pl.when(pl.program_id(0) == pl.num_programs(0) - 1)
        def _():
            a = dqkv[...]
            pack_pair(pack_ref, 0, a[:, 0:DP], a[:, DP : 2 * DP])
            pack_pair(pack_ref, PAIR, a[:, 2 * DP : 3 * DP], dwo)
            pack_norms(pack_ref, 3 * PAIR, [dnp[0], dnp[1]])


def feature_backward(x, qkv, p, of, n, g1t, yt, wqkvT, woT, np8, perm, row0, rows, R=16, U=2, slots=None, prev=None, packed=0):
    b0 = row0 // R
    nat = lambda w: pl.BlockSpec((R, FP, w), lambda i: (i + b0, 0, 0))
    turned = pl.BlockSpec((FP, R, DP), lambda i: (0, i + b0, 0))
    real = pl.BlockSpec((R, F, D), lambda i: (i + b0, 0, 0))
    accs = [shape((DP, 3 * DP), F32), shape((DP, DP), F32), shape((2, 8, DP), F32)]
    ins = [x, qkv, p, of, n, g1t, yt]
    specs = [real, nat(3 * DP), nat(H * FP), nat(DP), nat(DP), turned, turned]
    out_shape = [shape((x.shape[0], F, D), F32), shape((x.shape[0], F, D))]
    out_specs = [real, real]
    scratch = [
        pltpu.VMEM((R, FP, DP), F32),
        pltpu.VMEM((R, FP, DP), BF),
        pltpu.VMEM((R * FP, 3 * DP), BF),
        pltpu.VMEM((R * FP, DP), BF),
    ]
    SL = 0
    alias = {}
    shared = [wqkvT, woT, np8, perm]
    if slots is not None:
        SL = slots[0].shape[1]
        shared = list(slots) + shared
    ins += shared
    specs += [whole(a) for a in shared]
    if prev is not None:
        cg, y, *acc = prev
        ins += list(acc) + [cg, y]
        specs += [whole(a) for a in acc] + [pl.BlockSpec(memory_space=pl.ANY)] * 2
        alias = {len(ins) - 2: 0, len(ins) - 1: 1}
        out_shape.append(shape((packed, 128)))
        out_specs.append(pl.BlockSpec((packed, 128), lambda i: (0, 0)))
        scratch += [pltpu.VMEM(a.shape, F32) for a in accs]
    else:
        out_shape += accs
        out_specs += [whole(a) for a in accs]
    return pl.pallas_call(
        functools.partial(backward_kernel, R, U, SL),
        grid=(rows // R,),
        in_specs=specs,
        out_specs=out_specs,
        out_shape=out_shape,
        input_output_aliases=alias,
        scratch_shapes=scratch,
        compiler_params=params(),
        name="feature_backward",
    )(*ins)


def sum_kernel(parts_ref, out_ref):
    total = parts_ref[0].astype(F32)
    for i in range(1, parts_ref.shape[0]):
        total = total + parts_ref[i].astype(F32)
    out_ref[...] = total.astype(BF)


def sum_over_devices(packed, n):
    axes = ("table", "rows")
    rows = packed.shape[0] // n
    parts = lax.all_to_all(packed.reshape(n, rows, 128), axes, 0, 0)
    own = pl.pallas_call(
        sum_kernel, out_shape=shape((rows, 128)), compiler_params=params(), name="sum_parts"
    )(parts)
    copies = jnp.broadcast_to(own[None], (n, rows, 128))
    return lax.all_to_all(copies, axes, 0, 0).reshape(n * rows, 128)


def to_row(c):
    return jnp.broadcast_to(c, (c.shape[0], 128)).T[0:1]


def to_col(r):
    return jnp.broadcast_to(r, (128, r.shape[1])).T[:, 0:1]


def clipped(update, weight, count):
    def total(v):
        return jnp.sum(jnp.sum(v, 0, keepdims=True), 1, keepdims=True)

    rms = jnp.sqrt(total(update * update) * (1.0 / count))
    weight_rms = jnp.sqrt(total(weight * weight) * (1.0 / count))
    return update * (RATE * jnp.maximum(0.001, weight_rms) / jnp.maximum(1.0, rms / CLIP))


def optimizer_kernel(
    mid_ref, tail_ref, proj_ref, outw_ref, in_ref, hid_ref, norm_ref, sr_ref, sc_ref, mm_ref, mh_ref, ns_ref,
    proj_g, out_g, in_g, hid_g, norm_g, proj_n, out_n, in_n, hid_n, norm_n, sr_n, sc_n, mm_n, mh_n, ns_n,
):
    decay = 1.0 - STEP ** (-0.8)

    def stats(grad, col_old, row_old):
        square = grad * grad + 1e-30
        a, b = grad.shape
        over_sub = decay * row_old + (1.0 - decay) * (jnp.sum(square, 0, keepdims=True) * (1.0 / a))
        over_lane = decay * col_old + (1.0 - decay) * (jnp.sum(square, 1, keepdims=True) * (1.0 / b))
        return over_lane, over_sub

    def scaled(grad, col, row, mean):
        return grad * lax.rsqrt(col * (1.0 / mean)) * lax.rsqrt(row)

    def square_pair(ref, at):
        both = ref[at + 2 * D : at + 3 * D].astype(F32)
        a = jnp.concatenate([ref[at : at + D].astype(F32), both[:, 0:64]], 1)
        b = jnp.concatenate([ref[at + D : at + 2 * D].astype(F32), both[:, 64:128]], 1)
        return a, b

    wq, wk = square_pair(tail_ref, 0)
    wv, wo = square_pair(tail_ref, PAIR)
    wk2, wv2 = square_pair(tail_ref, 2 * PAIR)
    wq2, wo2 = square_pair(mid_ref, 12 * D)
    for i, grad in enumerate((wq, wk, wv, wq2, wk2, wv2, wo, wo2)):
        g_ref, n_ref, w_ref, j = (proj_g, proj_n, proj_ref, i) if i < 6 else (out_g, out_n, outw_ref, i - 6)
        g_ref[j] = grad
        col, row = stats(grad, to_col(sr_ref[i : i + 1, :]), sc_ref[i : i + 1, :])
        sr_n[i : i + 1, :] = to_row(col)
        sc_n[i : i + 1, :] = row
        mean = jnp.sum(col, 0, keepdims=True) * (1.0 / D)
        w = w_ref[j]
        n_ref[j] = w - clipped(scaled(grad, col, row, mean), w, D * D)

    def wide(at):
        return jnp.concatenate([mid_ref[at + D * j : at + D * j + D].astype(F32) for j in range(6)], 1)

    grad = wide(0)
    in_g[...] = grad
    col, row = stats(grad, to_col(mm_ref[0:1, :]), mh_ref[0:1, :])
    mm_n[0:1, :] = to_row(col)
    mh_n[0:1, :] = row
    mean = jnp.sum(col, 0, keepdims=True) * (1.0 / D)
    w = in_ref[...]
    in_n[...] = w - clipped(scaled(grad, col, row, mean), w, D * FF)
    grad = wide(6 * D)
    hid_g[...] = grad.T
    col, row = stats(grad, to_col(mm_ref[1:2, :]), mh_ref[1:2, :])
    mm_n[1:2, :] = to_row(col)
    mh_n[1:2, :] = row
    mean = jnp.sum(row, 1, keepdims=True) * (1.0 / FF)
    w = hid_ref[...]
    update = (grad * lax.rsqrt(col) * lax.rsqrt(row * (1.0 / mean))).T
    hid_n[...] = w - clipped(update, w, D * FF)

    pieces = []
    for ref, at, count in ((tail_ref, 3 * PAIR, 2), (mid_ref, 12 * D + PAIR, 4)):
        v = ref[at : at + 16].astype(F32)
        for i in range(count):
            pieces.append(jnp.concatenate([v[2 * i : 2 * i + 1], v[2 * i + 1 : 2 * i + 2, 0:64]], 1))
    grad = jnp.concatenate(pieces, 0)
    norm_g[...] = grad
    second = decay * ns_ref[...] + (1.0 - decay) * (grad * grad + 1e-30)
    ns_n[...] = second
    update = grad * lax.rsqrt(second)
    rms = jnp.sqrt(jnp.sum(update * update, 1, keepdims=True) * (1.0 / D))
    w = norm_ref[...]
    w_rms = jnp.sqrt(jnp.sum(w * w, 1, keepdims=True) * (1.0 / D))
    norm_n[...] = w - update * (RATE * jnp.maximum(0.001, w_rms) / jnp.maximum(1.0, rms / CLIP))


def optimizer(mid, tail, *state):
    proj, outw, w_in, w_out, norms, sr, sc, ms, hs, ns = state
    order = [proj, outw, w_in, w_out, norms, proj, outw, w_in, w_out, norms, sr, sc, ms, hs, ns]
    return pl.pallas_call(
        optimizer_kernel,
        out_shape=[shape(a.shape, F32) for a in order],
        compiler_params=params(),
        name="optimizer",
    )(mid, tail, *state)


def on_device(n, cells, cotangent, train_count, key_mask, train_order, *state):
    proj, outw, w_in, w_out, norms = state[:5]
    x = cells[0]
    rows_here = x.shape[0]
    unit = 8 * n
    tail_rows = -(-TAIL // unit) * unit
    mid_rows = -(-MID // unit) * unit
    perm = perm_matrix()
    (wqkv, wqkvT, wo, woT, wkv2, wk2T, wv2T, wq2, wq2T, wo2, wo2T, w1, w1T, w2, w2T, np8) = prepare(
        proj, outw, w_in, w_out, norms
    )
    own_kv = slot_keys(train_count, key_mask, train_order, x, wqkv, wo, wkv2, np8)
    shards = lax.axis_size("rows")
    copies = jnp.broadcast_to(own_kv[None], (shards,) + own_kv.shape)
    kv = lax.all_to_all(copies, "rows", 0, 0).reshape((-1,) + own_kv.shape[1:])
    nt, nn, qkv, p, of = feature_forward(x, wqkv, wo, perm)
    ct = to_columns(cotangent[0], perm)
    kt, vt, bias = gathered_columns(kv, perm)
    ws = (wq2, wq2T, wo2, wo2T, w1, w1T, w2, w2T)
    yt, g1t, dk, dv, mid = item_and_dense(nt, ct, kt, vt, bias, ws, np8, mid_rows)
    parts = slot_parts(dk, dv, perm).reshape((shards,) + own_kv.shape)
    parts = lax.all_to_all(parts, "rows", 0, 0)
    mid = sum_over_devices(mid, n)
    R = 16
    args = (x, qkv, p, of, nn, g1t, yt, wqkvT, woT, np8, perm)
    prev = feature_backward(*args, row0=R, rows=rows_here - R, R=R)
    cg, y, tail = feature_backward(
        *args, row0=0, rows=R, R=R, slots=(parts, wk2T, wv2T), prev=prev, packed=tail_rows
    )
    tail = sum_over_devices(tail, n)
    return (y[None], cg[None], *optimizer(mid, tail, *state))


def solution(mesh):
    n = int(mesh.shape["table"] * mesh.shape["rows"])
    cells = P("table", "rows", None, None)
    return jax.shard_map(
        functools.partial(on_device, n),
        mesh=mesh,
        in_specs=(cells, cells, P("table"), P("table", "rows"), P("table", "rows")) + (P(),) * 10,
        out_specs=(cells, cells) + (P(),) * 15,
        check_vma=False,
    )
```

time: 2410 us -> 524 us (0.22)
  blocking collectives: 1040 us -> 71.2 us
  local copies, waits for them, and re-layouts: 538 us -> 41.7 us
  Pallas kernels: 0 us -> 346 us
  matrix products: 329 us -> 0 us
  waiting for transfers between devices: 345 us -> 40.8 us
  other arithmetic: 124 us -> 0 us
    all_gather x28 -> x0, blocking collectives: 975 us -> none  [the longest x7 262 us: on_device(): lax.all_gather(lse_block.astype(jnp.bfloat16), 'rows', axis=2, tiled=True)]
    pallas_call x0 -> x12, Pallas kernels: none -> 346 us  [the longest x1 185 us: item_and_dense(): pl.pallas_call(functools.partial(item_kernel, FB, RW, keys, CH), grid=(pl...]
    dot_general x84 -> x0, matrix products: 312 us -> none  [the longest x20 114 us: product(): return jnp.dot(left, right, preferred_element_type=jnp.float32)]
    all_gather x14 -> x0, waiting for transfers between devices: 218 us -> none  [the longest x7 138 us: on_device(): lax.all_gather(grad_block, 'rows', axis=0, tiled=True)]
    reshape x56 -> x0, local copies, waits for them, and re-layouts: 184 us -> none  [the longest x35 119 us: split_heads(): return value.reshape(value.shape[:-1] + (HEADS, HEAD))]
    psum x1 -> x0, waiting for transfers between devices: 127 us -> none  [on_device(): lax.psum((proj_grad, out_grad, in_grad, hid_grad, norm_grad), ('table', '...]
    all_gather x35 -> x0, local copies, waits for them, and re-layouts: 122 us -> none  [the longest x7 43.4 us: on_device(): lax.all_gather(query_block, 'rows', axis=0, tiled=True)]
    slice x33 -> x0, local copies, waits for them, and re-layouts: 100 us -> none  [the longest x8 40.4 us: on_device(): query_item[:, columns]]
  transfers between devices with their start and end apart: 15 -> 5, of which waited for: 5 -> 4; matrix products, arithmetic and copies ran while one was open for 29% -> 4% of each run, Pallas kernels for 0% -> 26%
where the time goes in v1:
time: 524 us; the launch traced here: 522 us
  Pallas kernels  346 us (66%)
  blocking collectives  71.2 us (14%)
  local copies, waits for them, and re-layouts  41.7 us (8%)
  waiting for transfers between devices  40.8 us (8%)
  starting transfers between devices  21.2 us (4%)
    pallas_call x1, Pallas kernels, item_and_dense(): pl.pallas_call(functools.partial(item_kernel, FB, RW, keys, CH), grid=(pl...  185 us
    pallas_call x2, Pallas kernels, feature_backward(): pl.pallas_call(functools.partial(backward_kernel, R, U, SL), grid=(rows /...  80.1 us
    all_to_all x1, blocking collectives, on_device(): parts = lax.all_to_all(parts, 'rows', 0, 0)  71.2 us
    pallas_call x1, Pallas kernels, feature_forward(): pl.pallas_call(functools.partial(forward_kernel, R, U), grid=(rows // R,)...  44.2 us
    unnamed x17, local copies, waits for them, and re-layouts  35.6 us
    all_to_all x2, waiting for transfers between devices, sum_over_devices(): return lax.all_to_all(copies, axes, 0, 0).reshape(n * rows, 128)  20.6 us
    all_to_all x2, waiting for transfers between devices, sum_over_devices(): parts = lax.all_to_all(packed.reshape(n, rows, 128), axes, 0, 0)  13.1 us
  transfers between devices with their start and end apart: 5, of which 4 were waited for; matrix products, arithmetic and copies ran while one was open for 4% of the time, Pallas kernels for 26%

profile of v1, /device:TPU:0, one launch (start us, length us, event | category | flops | bytes accessed | tf_op | source)
XLA Modules:
  0.0 522.1 jit_solution(13634115940357953314)
XLA Ops:
  1.3 2.2 copy.36.w_out.hid_ref
  3.5 6.0 %copy.35 = bf16[1,64,119,192]{3,2,1,0:T(8,128)(2,1)} copy(bf16[1,64,119,192]{2,3,1,0:T(8,128)(2,1)} %param.16) | data formatting | bytes 5849088 | tf_op args[0]
  9.5 3.9 weights.1
  13.4 4.1 slot_keys.1
  17.5 2.8 broadcast_in_dim.10
  20.4 7.3 %all-to-all-start = ((bf16[8,4,120,384]{3,2,1,0:T(8,128)(2,1)}), bf16[8,4,120,384]{3,2,1,0:T(8,128)(2,1)S(1)}, u32[]{:S(2)}, u32[]{:S(2)}) async-start(bf16[8,4,120,384]{3,2,1,0:T(8,128)(2,1)} %broadcast_in_dim.10), calls=%async_computation | async-start | bytes 5898240 | tf_op jit(solution)/shard_map/all_to_all | solution.py:853
  27.6 6.0 %copy.37 = bf16[1,64,119,192]{3,2,1,0:T(8,128)(2,1)} copy(bf16[1,64,119,192]{2,3,1,0:T(8,128)(2,1)} %param.17) | data formatting | bytes 5849088 | tf_op args[1]
  33.6 44.2 %feature_forward.1 = (bf16[128,64,256]{2,1,0:T(8,128)(2,1)}, bf16[64,128,256]{2,1,0:T(8,128)(2,1)}, bf16[64,128,768]{2,1,0:T(8,128)(2,1)}, bf16[64,128,768]{2,1,0:T(8,128)(2,1)}, bf16[64,128,256]{2,1,0:T(8,128)(2,1)}) custom-call(bf16[64,119,192]{2,1,0:T(8,128)(2,1)} %bitcast.11, bf16[256,768]{1,0:T(8,128)(2,1)} %get-tuple-element.69.wqkv_ref, ...), custom_call_target="tpu_custom_call" | custom-call | tf_op jit(solution)/shard_map/feature_forward/pallas_call | solution.py:267
  77.8 9.1 %to_columns.1.ct_ref = bf16[128,64,256]{2,1,0:T(8,128)(2,1)} custom-call(bf16[64,119,192]{2,1,0:T(8,128)(2,1)} %bitcast.15, bf16[256,256]{1,0:T(8,128)(2,1)} %constant.2.clone.perm_ref.rest_3_.rest_6_), custom_call_target="tpu_custom_call" | custom-call | tf_op jit(solution)/shard_map/to_columns/pallas_call | solution.py:306
  86.9 7.2 %all-to-all-done = bf16[8,4,120,384]{3,2,1,0:T(8,128)(2,1)S(1)} async-done(((bf16[8,4,120,384]{3,2,1,0:T(8,128)(2,1)}), bf16[8,4,120,384]{3,2,1,0:T(8,128)(2,1)S(1)}, u32[]{:S(2)}, u32[]{:S(2)}) %all-to-all-start) | async-done | bytes 2949152 | tf_op jit(solution)/shard_map/all_to_all | solution.py:853
  94.1 0.0 copy-start
  94.1 1.6 copy-done
  95.7 4.5 gathered_columns.1
  100.3 184.5 %item_and_dense.1 = (bf16[128,64,256]{2,1,0:T(8,128)(2,1)}, bf16[128,64,256]{2,1,0:T(8,128)(2,1)}, bf16[128,32,256]{2,1,0:T(8,128)(2,1)}, bf16[128,32,256]{2,1,0:T(8,128)(2,1)}, bf16[3072,128]{1,0:T(8,128)(2,1)}) custom-call(bf16[128,64,256]{2,1,0:T(8,128)(2,1)} %get-tuple-element.75.nt_ref, bf16[128,64,256]{2,1,0:T(8,128)(2,1)} %to_columns.1.ct_ref, ...), custom_call_target="tpu_custom_call" | custom-call | tf_op jit(solution)/shard_map/item_and_dense/pallas_call | solution.py:532
  284.8 4.3 slot_parts.1
  289.1 71.2 %all_to_all.30.rest_0_ = bf16[8,4,120,384]{3,2,1,0:T(8,128)(2,1)} all-to-all(bf16[8,4,120,384]{3,2,1,0:T(8,128)(2,1)} %bitcast.17), channel_id=1, replica_groups=mesh['table'=4,'rows'=8] {'rows'}, dimensions={0} | all-to-all | bytes 5898240 | tf_op jit(solution)/shard_map/all_to_all | solution.py:860
  360.3 3.0 all-to-all-start.2
  363.3 56.0 %feature_backward.2 = (f32[64,119,192]{2,1,0:T(8,128)}, bf16[64,119,192]{2,1,0:T(8,128)(2,1)}, f32[256,768]{1,0:T(8,128)}, f32[256,256]{1,0:T(8,128)}, f32[2,8,256]{2,1,0:T(8,128)}) custom-call(bf16[64,119,192]{2,1,0:T(8,128)(2,1)} %bitcast.12, bf16[64,128,768]{2,1,0:T(8,128)(2,1)} %get-tuple-element.71.qkv_ref, ...), custom_call_target="tpu_custom_call" | custom-call | tf_op jit(solution)/shard_map/feature_backward/pallas_call | solution.py:707
  419.3 24.1 %feature_backward.3 = (f32[64,119,192]{2,1,0:T(8,128)}, bf16[64,119,192]{2,1,0:T(8,128)(2,1)}, bf16[1792,128]{1,0:T(8,128)(2,1)}) custom-call(bf16[64,119,192]{2,1,0:T(8,128)(2,1)} %bitcast.13, bf16[64,128,768]{2,1,0:T(8,128)(2,1)} %get-tuple-element.71.qkv_ref, ...), custom_call_target="tpu_custom_call", output_to_operand_aliasing={{0}: (17, {}), {1}: (18, {})} | custom-call | tf_op jit(solution)/shard_map/feature_backward/pallas_call | solution.py:707
  443.4 0.0 all-to-all-done.2.parts_ref
  443.4 0.0 copy-start.2
  443.4 5.7 %all-to-all-start.4 = ((bf16[32,56,128]{2,1,0:T(8,128)(2,1)}), bf16[32,56,128]{2,1,0:T(8,128)(2,1)S(1)}, u32[]{:S(2)}, u32[]{:S(2)}) async-start(bf16[32,56,128]{2,1,0:T(8,128)(2,1)} %bitcast.21), calls=%async_computation.4 | async-start | bytes 917504 | tf_op jit(solution)/shard_map/all_to_all | solution.py:730
  449.1 0.0 copy-done.2
  449.1 1.9 sum_parts.2
  451.0 13.1 %all-to-all-done.4.parts_ref = bf16[32,56,128]{2,1,0:T(8,128)(2,1)S(1)} async-done(((bf16[32,56,128]{2,1,0:T(8,128)(2,1)}), bf16[32,56,128]{2,1,0:T(8,128)(2,1)S(1)}, u32[]{:S(2)}, u32[]{:S(2)}) %all-to-all-start.4) | async-done | bytes 458784 | tf_op jit(solution)/shard_map/all_to_all | solution.py:730
  464.0 0.0 copy-start.3
  464.0 1.7 broadcast_in_dim.13
  465.8 2.6 all-to-all-start.3
  468.4 0.0 copy-done.3
  468.4 1.7 sum_parts.3
  470.1 20.3 %all-to-all-done.3 = bf16[32,96,128]{2,1,0:T(8,128)(2,1)S(1)} async-done(((bf16[32,96,128]{2,1,0:T(8,128)(2,1)}), bf16[32,96,128]{2,1,0:T(8,128)(2,1)S(1)}, u32[]{:S(2)}, u32[]{:S(2)}) %all-to-all-start.3) | async-done | bytes 786464 | tf_op jit(solution)/shard_map/all_to_all | solution.py:735
  490.4 0.0 copy-start.1
  490.4 1.5 broadcast_in_dim.28
  491.9 2.6 all-to-all-start.5
  494.5 6.0 %copy.39 = bf16[1,64,119,192]{2,3,1,0:T(8,128)(2,1)} copy(bf16[1,64,119,192]{3,2,1,0:T(8,128)(2,1)} %bitcast.16) | data formatting | bytes 5849088
  500.5 0.0 copy-done.1
  500.5 8.6 %copy.40 = f32[1,64,119,192]{2,3,1,0:T(8,128)} copy(f32[1,64,119,192]{3,2,1,0:T(8,128)} %bitcast.14) | data formatting | bytes 11698176
  509.2 0.3 all-to-all-done.5
  509.5 0.0 copy-start.4
  509.5 0.8 copy-done.4
  510.2 7.5 %optimizer.1 = (f32[6,192,192]{2,1,0:T(8,128)}, f32[2,192,192]{2,1,0:T(8,128)}, f32[192,768]{1,0:T(8,128)}, f32[768,192]{1,0:T(8,128)}, f32[6,192]{1,0:T(8,128)}...) custom-call(bf16[3072,128]{1,0:T(8,128)(2,1)} %bitcast.19, ...), custom_call_target="tpu_custom_call" | custom-call | tf_op jit(solution)/shard_map/optimizer/pallas_call | solution.py:831
  517.7 2.2 copy.41
  519.9 2.2 copy.42
Async XLA Ops:
  20.4 73.7 %all-to-all-start = ((bf16[8,4,120,384]{3,2,1,0:T(8,128)(2,1)}), bf16[8,4,120,384]{3,2,1,0:T(8,128)(2,1)S(1)}, u32[]{:S(2)}, u32[]{:S(2)}) async-start(bf16[8,4,120,384]{3,2,1,0:T(8,128)(2,1)} %broadcast_in_dim.10), calls=%async_computation | async-start | bytes 5898240 | tf_op jit(solution)/shard_map/all_to_all | solution.py:853
  94.1 1.6 copy-start
  360.3 83.1 %all-to-all-start.2 = ((bf16[32,96,128]{2,1,0:T(8,128)(2,1)}), bf16[32,96,128]{2,1,0:T(8,128)(2,1)S(1)}, u32[]{:S(2)}, u32[]{:S(2)}) async-start(bf16[32,96,128]{2,1,0:T(8,128)(2,1)} %bitcast.6), calls=%async_computation.2 | async-start | bytes 1572864 | tf_op jit(solution)/shard_map/all_to_all | solution.py:730
  443.4 5.7 %copy-start.2 = (bf16[32,96,128]{2,1,0:T(8,128)(2,1)}, bf16[32,96,128]{2,1,0:T(8,128)(2,1)S(1)}, u32[]{:S(2)}) copy-start(bf16[32,96,128]{2,1,0:T(8,128)(2,1)S(1)} %all-to-all-done.2.parts_ref) | copy-start | bytes 2359300
  443.4 20.6 %all-to-all-start.4 = ((bf16[32,56,128]{2,1,0:T(8,128)(2,1)}), bf16[32,56,128]{2,1,0:T(8,128)(2,1)S(1)}, u32[]{:S(2)}, u32[]{:S(2)}) async-start(bf16[32,56,128]{2,1,0:T(8,128)(2,1)} %bitcast.21), calls=%async_computation.4 | async-start | bytes 917504 | tf_op jit(solution)/shard_map/all_to_all | solution.py:730
  464.0 4.4 copy-start.3
  465.8 24.6 %all-to-all-start.3 = ((bf16[32,96,128]{2,1,0:T(8,128)(2,1)}), bf16[32,96,128]{2,1,0:T(8,128)(2,1)S(1)}, u32[]{:S(2)}, u32[]{:S(2)}) async-start(bf16[32,96,128]{2,1,0:T(8,128)(2,1)} %broadcast_in_dim.13), calls=%async_computation.3 | async-start | bytes 1572864 | tf_op jit(solution)/shard_map/all_to_all | solution.py:735
  490.4 10.2 %copy-start.1 = (bf16[32,96,128]{2,1,0:T(8,128)(2,1)}, bf16[32,96,128]{2,1,0:T(8,128)(2,1)S(1)}, u32[]{:S(2)}) copy-start(bf16[32,96,128]{2,1,0:T(8,128)(2,1)S(1)} %all-to-all-done.3) | copy-start | bytes 2359300
  491.9 17.6 %all-to-all-start.5 = ((bf16[32,56,128]{2,1,0:T(8,128)(2,1)}), bf16[32,56,128]{2,1,0:T(8,128)(2,1)S(1)}, u32[]{:S(2)}, u32[]{:S(2)}) async-start(bf16[32,56,128]{2,1,0:T(8,128)(2,1)} %broadcast_in_dim.28), calls=%async_computation.5 | async-start | bytes 917504 | tf_op jit(solution)/shard_map/all_to_all | solution.py:735
  509.5 0.8 copy-start.4

commit v2 on v1

--- a/solution.py
+++ b/solution.py
@@ -94,6 +94,10 @@
 
 def params(mib=58):
     return pltpu.CompilerParams(vmem_limit_bytes=mib << 20)
+
+
+def cost(us):
+    return pl.CostEstimate(flops=int(us * 1.1e9), bytes_accessed=int(us * 1e6), transcendentals=0)
 
 
 def perm_matrix():
@@ -159,7 +163,7 @@
         shape((DP, FF)),
         shape((8, DP), F32),
     ]
-    return pl.pallas_call(prep_kernel, out_shape=outs, compiler_params=params(), name="weights")(
+    return pl.pallas_call(prep_kernel, out_shape=outs, compiler_params=params(), cost_estimate=cost(4), name="weights")(
         proj, outw, w_in, w_out, norms
     )
 
@@ -221,7 +225,7 @@
         out_shape=shape((SL, FS, 2 * D)),
         scratch_shapes=[pltpu.VMEM((SL * FP, DP), BF)],
         compiler_params=params(),
-        name="slot_keys",
+        cost_estimate=cost(4), name="slot_keys",
     )(count, mask, order, cells, wqkv, wo, wkv2, np8)
 
 
@@ -284,7 +288,7 @@
         ],
         scratch_shapes=[pltpu.VMEM((U * FP, DP), BF)],
         compiler_params=params(),
-        name="feature_forward",
+        cost_estimate=cost(44), name="feature_forward",
     )(cells, wqkv, wo, perm)
 
 
@@ -311,7 +315,7 @@
         out_shape=shape((FP, rows, DP)),
         scratch_shapes=[pltpu.VMEM((16, FP, DP), BF)],
         compiler_params=params(),
-        name="to_columns",
+        cost_estimate=cost(9), name="to_columns",
     )(x, perm)
 
 
@@ -341,7 +345,7 @@
         out_shape=[shape((FP, keys, DP)), shape((FP, keys, DP)), shape((keys, 128), F32)],
         scratch_shapes=[pltpu.VMEM((16, FP, 2 * D), BF)],
         compiler_params=params(),
-        name="gathered_columns",
+        cost_estimate=cost(4), name="gathered_columns",
     )(kv, perm)
 
 
@@ -370,7 +374,7 @@
         out_specs=pl.BlockSpec((16, FS, 2 * D), lambda i: (i, 0, 0)),
         out_shape=shape((keys, FS, 2 * D)),
         compiler_params=params(),
-        name="slot_parts",
+        cost_estimate=cost(4), name="slot_parts",
     )(dk, dv, perm)
 
 
@@ -555,7 +559,7 @@
             wide,
         ],
         compiler_params=params(),
-        name="item_and_dense",
+        cost_estimate=cost(180), name="item_and_dense",
     )(nt, ct, kt, vt, bias, *ws, np8)
 
 
@@ -713,7 +717,7 @@
         input_output_aliases=alias,
         scratch_shapes=scratch,
         compiler_params=params(),
-        name="feature_backward",
+        cost_estimate=cost(60), name="feature_backward",
     )(*ins)
 
 
@@ -721,17 +725,18 @@
     total = parts_ref[0].astype(F32)
     for i in range(1, parts_ref.shape[0]):
         total = total + parts_ref[i].astype(F32)
-    out_ref[...] = total.astype(BF)
+    total = total.astype(BF)
+    for i in range(parts_ref.shape[0]):
+        out_ref[i] = total
 
 
 def sum_over_devices(packed, n):
     axes = ("table", "rows")
     rows = packed.shape[0] // n
     parts = lax.all_to_all(packed.reshape(n, rows, 128), axes, 0, 0)
-    own = pl.pallas_call(
-        sum_kernel, out_shape=shape((rows, 128)), compiler_params=params(), name="sum_parts"
+    copies = pl.pallas_call(
+        sum_kernel, out_shape=shape((n, rows, 128)), compiler_params=params(), cost_estimate=cost(2), name="sum_parts"
     )(parts)
-    copies = jnp.broadcast_to(own[None], (n, rows, 128))
     return lax.all_to_all(copies, axes, 0, 0).reshape(n * rows, 128)
 
 
@@ -832,7 +837,7 @@
         optimizer_kernel,
         out_shape=[shape(a.shape, F32) for a in order],
         compiler_params=params(),
-        name="optimizer",
+        cost_estimate=cost(8), name="optimizer",
     )(mid, tail, *state)
 
 
@@ -849,8 +854,7 @@
     )
     own_kv = slot_keys(train_count, key_mask, train_order, x, wqkv, wo, wkv2, np8)
     shards = lax.axis_size("rows")
-    copies = jnp.broadcast_to(own_kv[None], (shards,) + own_kv.shape)
-    kv = lax.all_to_all(copies, "rows", 0, 0).reshape((-1,) + own_kv.shape[1:])
+    kv = lax.all_gather(own_kv, "rows", axis=0, tiled=True)
     nt, nn, qkv, p, of = feature_forward(x, wqkv, wo, perm)
     ct = to_columns(cotangent[0], perm)
     kt, vt, bias = gathered_columns(kv, perm)

time: 524 us -> 461 us (0.88)
  blocking collectives: 71.2 us -> 0 us
  between operations: 1.39 us -> 14.8 us
  local copies, waits for them, and re-layouts: 41.7 us -> 33 us
  waiting for transfers between devices: 40.8 us -> 46.9 us
    all_to_all x1 -> x0, blocking collectives: 71.2 us -> none  [on_device(): parts = lax.all_to_all(parts, 'rows', 0, 0)]
    broadcast_in_dim x3 -> x0, local copies, waits for them, and re-layouts: 6.09 us -> none  [the longest x2 3.26 us: sum_over_devices(): copies = jnp.broadcast_to(own[None], (n, rows, 128))]
  transfers between devices with their start and end apart: 5 -> 6, of which waited for: 4 -> 5; matrix products, arithmetic and copies ran while one was open for 4% -> 4% of each run, Pallas kernels for 26% -> 30%
where the time goes in v2:
time: 461 us; the launch traced here: 460 us
  Pallas kernels  346 us (75%)
  waiting for transfers between devices  46.9 us (10%)
  local copies, waits for them, and re-layouts  33 us (7%)
  starting transfers between devices  18.9 us (4%)
  between operations  14.8 us (3%)
    pallas_call x1, Pallas kernels, item_and_dense(): pl.pallas_call(functools.partial(item_kernel, FB, RW, keys, CH), grid=(pl...  185 us
    pallas_call x2, Pallas kernels, feature_backward(): pl.pallas_call(functools.partial(backward_kernel, R, U, SL), grid=(rows /...  80 us
    pallas_call x1, Pallas kernels, feature_forward(): pl.pallas_call(functools.partial(forward_kernel, R, U), grid=(rows // R,)...  44.2 us
    unnamed x17, local copies, waits for them, and re-layouts  33 us
    all_to_all x2, waiting for transfers between devices, sum_over_devices(): return lax.all_to_all(copies, axes, 0, 0).reshape(n * rows, 128)  20.4 us
    all_to_all x2, waiting for transfers between devices, sum_over_devices(): parts = lax.all_to_all(packed.reshape(n, rows, 128), axes, 0, 0)  12.8 us
    all_to_all x1, waiting for transfers between devices, on_device(): parts = lax.all_to_all(parts, 'rows', 0, 0)  10.5 us
    all_to_all x2, starting transfers between devices, sum_over_devices(): parts = lax.all_to_all(packed.reshape(n, rows, 128), axes, 0, 0)  9.57 us
  transfers between devices with their start and end apart: 6, of which 5 were waited for; matrix products, arithmetic and copies ran while one was open for 4% of the time, Pallas kernels for 30%

profile of v2, /device:TPU:0, one launch (start us, length us, event | category | flops | bytes accessed | tf_op | source)
XLA Modules:
  0.0 460.1 jit_solution(5232756716810110347)
XLA Ops:
  7.2 0.0 all-gather.2.cloned.1.call-start
  7.9 2.2 copy.44.w_out.hid_ref
  10.1 6.0 %copy.43 = bf16[1,64,119,192]{3,2,1,0:T(8,128)(2,1)} copy(bf16[1,64,119,192]{2,3,1,0:T(8,128)(2,1)} %param.16) | data formatting | bytes 5849088 | tf_op args[0]
  16.1 3.9 weights.1
  20.0 0.0 copy-start
  20.0 4.3 slot_keys.1
  24.3 0.0 all-gather.2.cloned.1.call-update
  24.3 0.0 copy-done
  24.3 5.0 %copy.45 = bf16[1,64,119,192]{3,2,1,0:T(8,128)(2,1)} copy(bf16[1,64,119,192]{2,3,1,0:T(8,128)(2,1)S(1)} %copy-done) | data formatting | bytes 5849088 | tf_op args[1]
  29.3 9.1 %to_columns.1.ct_ref = bf16[128,64,256]{2,1,0:T(8,128)(2,1)} custom-call(bf16[64,119,192]{2,1,0:T(8,128)(2,1)} %bitcast.15, bf16[256,256]{1,0:T(8,128)(2,1)} %constant.2.clone.perm_ref.rest_3_.rest_6_), custom_call_target="tpu_custom_call" | custom-call | flops 9900000256 | bytes 9000000 | tf_op jit(solution)/shard_map/to_columns/pallas_call | solution.py:310
  38.4 44.2 %feature_forward.1 = (bf16[128,64,256]{2,1,0:T(8,128)(2,1)}, bf16[64,128,256]{2,1,0:T(8,128)(2,1)}, bf16[64,128,768]{2,1,0:T(8,128)(2,1)}, bf16[64,128,768]{2,1,0:T(8,128)(2,1)}, bf16[64,128,256]{2,1,0:T(8,128)(2,1)}) custom-call(bf16[64,119,192]{2,1,0:T(8,128)(2,1)} %bitcast.11, bf16[256,768]{1,0:T(8,128)(2,1)} %get-tuple-element.69.wqkv_ref, ...), custom_call_target="tpu_custom_call" | custom-call | flops 48399998976 | bytes 44000000 | tf_op jit(solution)/shard_map/feature_forward/pallas_call | solution.py:271
  82.6 3.2 all-gather.2.cloned.1.call-done.kv_ref
  85.8 4.5 gathered_columns.1
  90.3 184.5 %item_and_dense.1 = (bf16[128,64,256]{2,1,0:T(8,128)(2,1)}, bf16[128,64,256]{2,1,0:T(8,128)(2,1)}, bf16[128,32,256]{2,1,0:T(8,128)(2,1)}, bf16[128,32,256]{2,1,0:T(8,128)(2,1)}, bf16[3072,128]{1,0:T(8,128)(2,1)}) custom-call(bf16[128,64,256]{2,1,0:T(8,128)(2,1)} %get-tuple-element.75.nt_ref, bf16[128,64,256]{2,1,0:T(8,128)(2,1)} %to_columns.1.ct_ref, ...), custom_call_target="tpu_custom_call" | custom-call | flops 198000001024 | bytes 180000000 | tf_op jit(solution)/shard_map/item_and_dense/pallas_call | solution.py:536
  274.9 4.3 slot_parts.1
  279.2 4.1 all-to-all-start
  283.3 56.0 %feature_backward.2 = (f32[64,119,192]{2,1,0:T(8,128)}, bf16[64,119,192]{2,1,0:T(8,128)(2,1)}, f32[256,768]{1,0:T(8,128)}, f32[256,256]{1,0:T(8,128)}, f32[2,8,256]{2,1,0:T(8,128)}) custom-call(bf16[64,119,192]{2,1,0:T(8,128)(2,1)} %bitcast.12, bf16[64,128,768]{2,1,0:T(8,128)(2,1)} %get-tuple-element.71.qkv_ref, ...), custom_call_target="tpu_custom_call" | custom-call | flops 65999998976 | bytes 60000000 | tf_op jit(solution)/shard_map/feature_backward/pallas_call | solution.py:711
  339.2 10.5 %all-to-all-done.rest_0_ = bf16[8,4,120,384]{3,2,1,0:T(8,128)(2,1)S(1)} async-done(((bf16[8,4,120,384]{3,2,1,0:T(8,128)(2,1)}), bf16[8,4,120,384]{3,2,1,0:T(8,128)(2,1)S(1)}, u32[]{:S(2)}, u32[]{:S(2)}) %all-to-all-start) | async-done | bytes 2949152 | tf_op jit(solution)/shard_map/all_to_all | solution.py:864
  349.8 0.0 copy-start.1
  349.8 3.8 all-to-all-start.1
  353.6 0.0 copy-done.1
  353.6 24.1 %feature_backward.3 = (f32[64,119,192]{2,1,0:T(8,128)}, bf16[64,119,192]{2,1,0:T(8,128)(2,1)}, bf16[1792,128]{1,0:T(8,128)(2,1)}) custom-call(bf16[64,119,192]{2,1,0:T(8,128)(2,1)} %bitcast.13, bf16[64,128,768]{2,1,0:T(8,128)(2,1)} %get-tuple-element.71.qkv_ref, ...), custom_call_target="tpu_custom_call", output_to_operand_aliasing={{0}: (17, {}), {1}: (18, {})} | custom-call | flops 65999998976 | bytes 60000000 | tf_op jit(solution)/shard_map/feature_backward/pallas_call | solution.py:711
  377.7 0.0 all-to-all-done.1.parts_ref
  377.7 5.8 %all-to-all-start.3 = ((bf16[32,56,128]{2,1,0:T(8,128)(2,1)}), bf16[32,56,128]{2,1,0:T(8,128)(2,1)S(1)}, u32[]{:S(2)}, u32[]{:S(2)}) async-start(bf16[32,56,128]{2,1,0:T(8,128)(2,1)} %bitcast.19), calls=%async_computation.3 | async-start | bytes 917504 | tf_op jit(solution)/shard_map/all_to_all | solution.py:736
  383.4 2.1 sum_parts.2
  385.6 12.8 %all-to-all-done.3.parts_ref = bf16[32,56,128]{2,1,0:T(8,128)(2,1)S(1)} async-done(((bf16[32,56,128]{2,1,0:T(8,128)(2,1)}), bf16[32,56,128]{2,1,0:T(8,128)(2,1)S(1)}, u32[]{:S(2)}, u32[]{:S(2)}) %all-to-all-start.3) | async-done | bytes 458784 | tf_op jit(solution)/shard_map/all_to_all | solution.py:736
  398.4 0.0 copy-start.4
  398.4 2.6 all-to-all-start.2
  401.0 0.0 copy-done.4
  401.0 1.9 sum_parts.3
  402.9 20.1 %all-to-all-done.2 = bf16[32,96,128]{2,1,0:T(8,128)(2,1)S(1)} async-done(((bf16[32,96,128]{2,1,0:T(8,128)(2,1)}), bf16[32,96,128]{2,1,0:T(8,128)(2,1)S(1)}, u32[]{:S(2)}, u32[]{:S(2)}) %all-to-all-start.2) | async-done | bytes 786464 | tf_op jit(solution)/shard_map/all_to_all | solution.py:740
  423.0 0.0 copy-start.2
  423.0 2.6 all-to-all-start.4
  425.6 6.0 %copy.47 = bf16[1,64,119,192]{2,3,1,0:T(8,128)(2,1)} copy(bf16[1,64,119,192]{3,2,1,0:T(8,128)(2,1)} %bitcast.14) | data formatting | bytes 5849088
  431.6 0.0 copy-done.2
  431.6 8.6 %copy.48 = f32[1,64,119,192]{2,3,1,0:T(8,128)} copy(f32[1,64,119,192]{3,2,1,0:T(8,128)} %bitcast.9) | data formatting | bytes 11698176
  440.3 0.3 all-to-all-done.4
  440.6 0.0 copy-start.3
  440.6 0.8 copy-done.3
  441.3 7.5 %optimizer.1 = (f32[6,192,192]{2,1,0:T(8,128)}, f32[2,192,192]{2,1,0:T(8,128)}, f32[192,768]{1,0:T(8,128)}, f32[768,192]{1,0:T(8,128)}, f32[6,192]{1,0:T(8,128)}...) custom-call(bf16[3072,128]{1,0:T(8,128)(2,1)} %bitcast.18, ...), custom_call_target="tpu_custom_call" | custom-call | flops 8800000000 | bytes 8000000 | tf_op jit(solution)/shard_map/optimizer/pallas_call | solution.py:836
  448.8 2.2 copy.49
  451.0 2.2 copy.50
Async XLA Ops:
  7.2 78.6 %all-gather.2.cloned.1.call-start = ((), (), s32[]{:S(2)}) async-start(), calls=%async_computation.5 | async-start | bytes 3317760 | tf_op jit(solution)/shard_map/all_gather | solution.py:857
  20.0 4.3 copy-start
  279.2 70.6 %all-to-all-start = ((bf16[8,4,120,384]{3,2,1,0:T(8,128)(2,1)}), bf16[8,4,120,384]{3,2,1,0:T(8,128)(2,1)S(1)}, u32[]{:S(2)}, u32[]{:S(2)}) async-start(bf16[8,4,120,384]{3,2,1,0:T(8,128)(2,1)} %bitcast.16), calls=%async_computation | async-start | bytes 5898240 | tf_op jit(solution)/shard_map/all_to_all | solution.py:864
  349.8 3.8 copy-start.1
  349.8 27.9 %all-to-all-start.1 = ((bf16[32,96,128]{2,1,0:T(8,128)(2,1)}), bf16[32,96,128]{2,1,0:T(8,128)(2,1)}, u32[]{:S(2)}, u32[]{:S(2)}) async-start(bf16[32,96,128]{2,1,0:T(8,128)(2,1)} %bitcast.17), calls=%async_computation.1 | async-start | bytes 1572864 | tf_op jit(solution)/shard_map/all_to_all | solution.py:736
  377.7 20.7 %all-to-all-start.3 = ((bf16[32,56,128]{2,1,0:T(8,128)(2,1)}), bf16[32,56,128]{2,1,0:T(8,128)(2,1)S(1)}, u32[]{:S(2)}, u32[]{:S(2)}) async-start(bf16[32,56,128]{2,1,0:T(8,128)(2,1)} %bitcast.19), calls=%async_computation.3 | async-start | bytes 917504 | tf_op jit(solution)/shard_map/all_to_all | solution.py:736
  398.4 2.6 copy-start.4
  398.4 24.6 %all-to-all-start.2 = ((bf16[32,96,128]{2,1,0:T(8,128)(2,1)}), bf16[32,96,128]{2,1,0:T(8,128)(2,1)S(1)}, u32[]{:S(2)}, u32[]{:S(2)}) async-start(bf16[32,96,128]{2,1,0:T(8,128)(2,1)} %sum_parts.2), calls=%async_computation.2 | async-start | bytes 1572864 | tf_op jit(solution)/shard_map/all_to_all | solution.py:740
  423.0 8.6 %copy-start.2 = (bf16[32,96,128]{2,1,0:T(8,128)(2,1)}, bf16[32,96,128]{2,1,0:T(8,128)(2,1)S(1)}, u32[]{:S(2)}) copy-start(bf16[32,96,128]{2,1,0:T(8,128)(2,1)S(1)} %all-to-all-done.2) | copy-start | bytes 2359300
  423.0 17.6 %all-to-all-start.4 = ((bf16[32,56,128]{2,1,0:T(8,128)(2,1)}), bf16[32,56,128]{2,1,0:T(8,128)(2,1)S(1)}, u32[]{:S(2)}, u32[]{:S(2)}) async-start(bf16[32,56,128]{2,1,0:T(8,128)(2,1)} %sum_parts.3), calls=%async_computation.4 | async-start | bytes 917504 | tf_op jit(solution)/shard_map/all_to_all | solution.py:740
  440.6 0.8 copy-start.3
Sparse Core Ops, SparseCore 0:
  24.4 61.3 all-gather.1

commit v3 on v2

--- a/solution.py
+++ b/solution.py
@@ -109,7 +109,7 @@
 
 
 def prep_kernel(
-    proj, outw, w_in, w_out, norms, wqkv, wqkvT, wo, woT, wkv2, wk2T, wv2T, wq2, wq2T, wo2, wo2T, w1, w1T, w2, w2T, np8
+    proj, outw, w_in, w_outT, norms, wqkv, wqkvT, wo, woT, wkv2, wk2T, wv2T, wq2, wq2T, wo2I, wo2, w1T, w1, w2T, w2, np8, vec
 ):
     zc = jnp.zeros((D, DP - D), F32)
     zr = jnp.zeros((DP - D, DP), BF)
@@ -123,27 +123,35 @@
         a, t = square(proj[i])
         wqkv[:, i * DP : (i + 1) * DP] = a
         wqkvT[i * DP : (i + 1) * DP, :] = t
-    for src, dst, dstT in ((outw[0], wo, woT), (proj[3], wq2, wq2T), (outw[1], wo2, wo2T)):
+    for src, dst, dstT in ((outw[0], wo, woT), (proj[3], wq2, wq2T)):
         a, t = square(src)
         dst[...] = a
         dstT[...] = t
+    a, t = square(outw[1])
+    wo2[...] = a[0:D]
+    wo2I[:, 0:DP] = t[0:D]
+    row = lax.broadcasted_iota(jnp.int32, (D, DP), 0)
+    wo2I[:, DP : 2 * DP] = jnp.where(row == lax.broadcasted_iota(jnp.int32, (D, DP), 1), 1.0, 0.0).astype(BF)
     a, t = square(proj[4])
     wk2T[...] = t
     a, t = square(proj[5])
     wv2T[...] = t
     wkv2[0:D, :] = jnp.concatenate([proj[4], proj[5]], 1).astype(BF)
     wkv2[D:DP, :] = jnp.zeros((DP - D, 2 * D), BF)
-    a = jnp.concatenate([w_in[...].astype(BF), jnp.zeros((DP - D, FF), BF)], 0)
+    zw = jnp.zeros((DP - D, FF), BF)
+    a = w_in[...].astype(BF)
     w1[...] = a
-    w1T[...] = a.T
-    a = jnp.concatenate([w_out[...], jnp.zeros((FF, DP - D), F32)], 1).astype(BF)
-    w2[...] = a
-    w2T[...] = a.T
+    w1T[...] = jnp.concatenate([a, zw], 0).T
+    a = w_outT[...].astype(BF)
+    w2T[...] = a
+    w2[...] = jnp.concatenate([a, zw], 0).T
     np8[...] = jnp.zeros((8, DP), F32)
     np8[0:6, 0:D] = norms[...]
-
-
-def prepare(proj, outw, w_in, w_out, norms):
+    for i in range(6):
+        vec[i] = jnp.broadcast_to(np8[i : i + 1, :], (128, DP)).T[0:D]
+
+
+def prepare(proj, outw, w_in, w_outT, norms):
     sq = shape((DP, DP))
     outs = [
         shape((DP, 3 * DP)),
@@ -155,17 +163,18 @@
         sq,
         sq,
         sq,
-        sq,
-        sq,
-        shape((DP, FF)),
+        shape((D, 2 * DP)),
+        shape((D, DP)),
         shape((FF, DP)),
+        shape((D, FF)),
+        shape((D, FF)),
         shape((FF, DP)),
-        shape((DP, FF)),
         shape((8, DP), F32),
+        shape((6, D, 128), F32),
     ]
-    return pl.pallas_call(prep_kernel, out_shape=outs, compiler_params=params(), cost_estimate=cost(4), name="weights")(
-        proj, outw, w_in, w_out, norms
-    )
+    return pl.pallas_call(
+        prep_kernel, out_shape=outs, compiler_params=params(), cost_estimate=cost(4), name="weights"
+    )(proj, outw, w_in, w_outT, norms)
 
 
 def feature_rows(x, wqkv, wo, masks, lane_ok, U, keep=None):
@@ -229,7 +238,7 @@
     )(count, mask, order, cells, wqkv, wo, wkv2, np8)
 
 
-def forward_kernel(R, U, x_ref, wqkv_ref, wo_ref, perm_ref, nt_ref, n_ref, qkv_ref, p_ref, of_ref, xs):
+def forward_kernel(R, U, x_ref, wqkv_ref, wo_ref, np_ref, perm_ref, nt_ref, n_ref, qkv_ref, p_ref, of_ref, xs, hs):
     @pl.when(pl.program_id(0) == 0)
     def _():
         xs[...] = jnp.zeros_like(xs)
@@ -249,29 +258,31 @@
             of_ref[r0 + u] = o
 
         n, rc = feature_rows(xs[...], wqkv_ref[...], wo_ref[...], masks, lane_ok, U, keep)
+        h = (n * np_ref[0:1, :] + np_ref[1:2, :]).astype(BF)
         n = jnp.where(lane >= D, rc, n).astype(BF)
         for u in range(U):
             n_ref[r0 + u] = n[u * FP : (u + 1) * FP]
+            hs[r0 + u] = h[u * FP : (u + 1) * FP]
         return carry
 
     lax.fori_loop(0, R // U, rows, 0)
 
     def turn(j, carry):
         f0 = pl.multiple_of(j * 16, 16)
-        block = n_ref[:, pl.ds(f0, 16), :].reshape(R * 16, DP)
+        block = hs[:, pl.ds(f0, 16), :].reshape(R * 16, DP)
         nt_ref[pl.ds(f0, 16)] = mm(perm_ref[...], block).astype(BF).reshape(16, R, DP)
         return carry
 
     lax.fori_loop(0, FP // 16, turn, 0)
 
 
-def feature_forward(cells, wqkv, wo, perm, R=16, U=4):
+def feature_forward(cells, wqkv, wo, np8, perm, R=16, U=4):
     rows = cells.shape[0]
     nat = lambda w: pl.BlockSpec((R, FP, w), lambda i: (i, 0, 0))
     return pl.pallas_call(
         functools.partial(forward_kernel, R, U),
         grid=(rows // R,),
-        in_specs=[pl.BlockSpec((R, F, D), lambda i: (i, 0, 0)), whole(wqkv), whole(wo), whole(perm)],
+        in_specs=[pl.BlockSpec((R, F, D), lambda i: (i, 0, 0)), whole(wqkv), whole(wo), whole(np8), whole(perm)],
         out_specs=[
             pl.BlockSpec((FP, R, DP), lambda i: (0, i, 0)),
             nat(DP),
@@ -286,10 +297,10 @@
             shape((rows, FP, H * FP)),
             shape((rows, FP, DP)),
         ],
-        scratch_shapes=[pltpu.VMEM((U * FP, DP), BF)],
+        scratch_shapes=[pltpu.VMEM((U * FP, DP), BF), pltpu.VMEM((R, FP, DP), BF)],
         compiler_params=params(),
         cost_estimate=cost(44), name="feature_forward",
-    )(cells, wqkv, wo, perm)
+    )(cells, wqkv, wo, np8, perm)
 
 
 def columns_kernel(x_ref, perm_ref, out_ref, xs):
@@ -387,180 +398,274 @@
 def pack_norms(ref, at, sums):
     rows = []
     for s in sums:
+        if s.shape[0] == D:
+            s = jnp.concatenate([s, jnp.zeros((DP - D, 128), F32)], 0).T
         v = jnp.sum(s, 0, keepdims=True)
         rows += [v[:, 0:128], v[:, 128:256]]
     rows.append(jnp.zeros((ref.shape[0] - at - len(rows), 128), F32))
     ref[at:] = jnp.concatenate(rows, 0).astype(BF)
 
 
-def item_kernel(
-    FB, RW, keys, CH, nt_ref, ct_ref, kt_ref, vt_ref, bias_ref, wq_ref, wqT_ref, wo_ref, woT_ref, w1_ref, w1T_ref,
-    w2_ref, w2T_ref, np_ref, y_ref, g1_ref, dk_ref, dv_ref, pack_ref, dwq, dwo, dw1, dw2, dnp, h1b, qs, pbs, oi, da2s,
-    dab, doi, dqs, h2b, dub, dbr, acts,
-):
-    M = FB * RW
-
-    @pl.when(pl.program_id(0) == 0)
+def half_masks():
+    lane = lax.broadcasted_iota(jnp.int32, (1, 128), 1)
+    return [jnp.where((lane >= E * h) & (lane < E * (h + 1)), 1.0, 0.0).astype(BF) for h in range(4)]
+
+def spread_halves(w, masks):
+    z = jnp.zeros((w.shape[0], 128), BF)
+    lo, hi = w[:, 0:128], w[:, 128:256]
+    return jnp.concatenate(
+        [jnp.concatenate([lo * masks[h], z], 1) for h in range(4)]
+        + [jnp.concatenate([z, hi * masks[h]], 1) for h in range(2)], 0)
+
+def mean0(a): return jnp.sum(a, 0, keepdims=True) * (1.0 / D)
+
+def norm_t(a):
+    c = a - mean0(a)
+    rc = lax.rsqrt(mean0(c * c) + 1e-5)
+    return c * rc, rc
+
+def norm_back_t(g, n, rc, gain):
+    dn = g * gain
+    return (dn - mean0(dn) - n * mean0(dn * n)) * rc
+
+def tall(a):
+    return jnp.concatenate([a, jnp.zeros((DP - D, a.shape[1]), a.dtype)], 0)
+
+def gelu_parts(u):
+    uu = u * u
+    th = jnp.tanh(u * (BF(C0) + BF(C0 * C1) * uu))
+    half = BF(0.5) + BF(0.5) * th
+    act = u * half
+    slope = half + act * (BF(1.0) - th) * (BF(C0) + BF(3.0 * C0 * C1) * uu)
+    return act, slope
+
+
+def weave(streams):
+    live=[[g,s,p] for g,s,p in streams]
+    turn=0
+    while live:
+        for it in list(live):
+            if turn>=it[1]:
+                for _ in range(it[2]):
+                    try: next(it[0])
+                    except StopIteration:
+                        live.remove(it); break
+        turn+=1
+
+def item_kernel(FB, RW, keys, OFF, WP, CC, WC,
+    ht_ref, ct_ref, kt_ref, vt_ref, bias_ref, wq_ref, wqT_ref, woI_ref, wo_ref, w1T_ref, w1_ref, w2T_ref, w2_ref, vec_ref,
+    y_ref, g1_ref, dk_ref, dv_ref, pack_ref, dwq, dwo, dw1, dw2, dnp,
+    hbTs, ois, hb2Ts, actss, dbTs, duss, dabTs, dqss, slp):
+    step = pl.program_id(0)
+    @pl.when(step == 0)
     def _():
         for ref in (dwq, dwo, dw1, dw2, dnp):
             ref[...] = jnp.zeros_like(ref)
-
-    masks = head_masks()
-    lane_ok = (lanes() < D).astype(F32)
-    g0, b0, g1, b1, g2, b2 = [np_ref[i : i + 1, :] for i in range(6)]
-    left = lax.broadcasted_iota(jnp.int32, (1, 2 * RW), 1) < RW
+        for ref in (hbTs, ois, hb2Ts, actss, dbTs, duss, dabTs, dqss):
+            ref[1] = jnp.zeros_like(ref[1])
+    cur = step % 2
+    masks = half_masks()
+    LW = 2 * RW
+    left = lax.broadcasted_iota(jnp.int32, (1, LW), 1) < RW
     HK = H * keys
-
-    def attend(j, carry):
-        s0 = pl.multiple_of(j * 2 * RW, 2 * RW)
-        n = nt_ref[pl.ds(2 * j, 2)].reshape(2 * RW, DP).astype(F32)
-        hb = (n * g0 + b0).astype(BF)
-        h1b[pl.ds(s0, 2 * RW)] = hb
-        q = mm(hb, wq_ref[...]).astype(BF)
-        qs[pl.ds(s0, 2 * RW)] = q
-        ka, kb = spread(kt_ref[2 * j], masks), spread(kt_ref[2 * j + 1], masks)
-        st = jnp.where(left, mm_nt(ka, q), mm_nt(kb, q))
-        st = st.reshape(H, keys, 2 * RW) + bias_ref[...][None]
-        mx = jnp.max(st, 1, keepdims=True)
-        e = jnp.exp2((st - mx) * SCALE2)
-        total = jnp.sum(e, 1, keepdims=True)
-        pb = (e * (1.0 / total)).reshape(HK, 2 * RW).astype(BF)
-        pbs[j] = pb
+    hbT, oi, hb2T, acts, dbT, dus, dabT, dqs = [r.at[cur] for r in (hbTs, ois, hb2Ts, actss, dbTs, duss, dabTs, dqss)]
+    def attend(j, out):
+        h = ht_ref[2 * j:2 * j + 2].reshape(LW, DP)
+        q = (mm(h, wq_ref[...]) * SCALE2).astype(BF)
+        yield
+        ks = [spread_halves(kt_ref[2 * j + c], masks) for c in range(2)]
+        hbT[:, j * LW:(j + 1) * LW] = h.T[0:D]
+        yield
+        st = jnp.where(left, mm_nt(ks[0], q), mm_nt(ks[1], q))
+        yield
+        vs = [spread_halves(vt_ref[2 * j + c], masks) for c in range(2)]
+        pbs = []
+        for hh in range(H):
+            s = st[hh * keys:(hh + 1) * keys] + bias_ref[...]
+            e = jnp.exp2(s - jnp.max(s, 0, keepdims=True))
+            pbs.append((e * (1.0 / jnp.sum(e, 0, keepdims=True))).astype(BF))
+            if hh % 2: yield
+        pb = jnp.concatenate(pbs, 0)
         pt = pb.T
-        va, vb = spread(vt_ref[2 * j], masks), spread(vt_ref[2 * j + 1], masks)
-        oi[pl.ds(s0, RW)] = mm(pt[:RW], va).astype(BF)
-        oi[pl.ds(s0 + RW, RW)] = mm(pt[RW:], vb).astype(BF)
-        return carry
-
-    lax.fori_loop(0, FB // 2, attend, 0)
-
-    def dense(j, carry):
-        gs2, bs2, gs1, bs1 = carry
-        s0 = pl.multiple_of(j * CH, CH)
-        cols = CH // RW
-        h1 = nt_ref[pl.ds(j * cols, cols)].reshape(CH, DP).astype(F32) * g0 + b0
-        n2, rc2 = layer_norm(h1 + mm(oi[pl.ds(s0, CH)], wo_ref[...]), lane_ok)
-        h2 = n2 * g1 + b1
-        hb = h2.astype(BF)
-        h2b[pl.ds(s0, CH)] = hb
-        u = mm(hb, w1_ref[...])
-        uu = u * u
-        th = jnp.tanh(u * (C0 + (C0 * C1) * uu))
-        half = 0.5 + 0.5 * th
-        act = (u * half).astype(BF)
-        acts[pl.ds(s0, CH)] = act
-        slope = half + (0.5 * u) * (1.0 - th * th) * (C0 + (3.0 * C0 * C1) * uu)
-        n3, rc3 = layer_norm(h2 + mm(act, w2_ref[...]), lane_ok)
-        y_ref[pl.ds(j * cols, cols)] = (n3 * g2 + b2).astype(BF).reshape(cols, RW, DP)
-        g = ct_ref[pl.ds(j * cols, cols)].reshape(CH, DP).astype(F32)
-        gs2 = gs2 + fold8(g * n3)
-        bs2 = bs2 + fold8(g)
-        d3 = norm_back(g, n3, rc3, g2, lane_ok)
-        db = d3.astype(BF)
-        dbr[pl.ds(s0, CH)] = db
-        du = (mm(db, w2T_ref[...]) * slope).astype(BF)
-        dub[pl.ds(s0, CH)] = du
-        dh2 = d3 + mm(du, w1T_ref[...])
-        gs1 = gs1 + fold8(dh2 * n2)
-        bs1 = bs1 + fold8(dh2)
-        d2 = norm_back(dh2, n2, rc2, g1, lane_ok)
-        da2s[pl.ds(s0, CH)] = d2
-        d2b = d2.astype(BF)
-        dab[pl.ds(s0, CH)] = d2b
-        doi[pl.ds(s0, CH)] = mm(d2b, woT_ref[...]).astype(BF)
-        return gs2, bs2, gs1, bs1
-
-    z = jnp.zeros((8, DP), F32)
-    gs2, bs2, gs1, bs1 = lax.fori_loop(0, M // CH, dense, (z, z, z, z))
-    dnp[0] += gs1
-    dnp[1] += bs1
-    dnp[2] += gs2
-    dnp[3] += bs2
-    zero = jnp.zeros((RW, DP), BF)
-
-    def back(j, carry):
-        s0 = pl.multiple_of(j * 2 * RW, 2 * RW)
-        q, do = qs[pl.ds(s0, 2 * RW)], doi[pl.ds(s0, 2 * RW)]
-        pb = pbs[j]
-        ka, kb = spread(kt_ref[2 * j], masks), spread(kt_ref[2 * j + 1], masks)
-        va, vb = spread(vt_ref[2 * j], masks), spread(vt_ref[2 * j + 1], masks)
-        dp = jnp.where(left, mm_nt(va, do), mm_nt(vb, do)).reshape(H, keys, 2 * RW)
-        p = pb.astype(F32).reshape(H, keys, 2 * RW)
-        off = jnp.sum(p * dp, 1, keepdims=True)
-        ds = (p * (dp - off)).reshape(HK, 2 * RW).astype(BF)
+        yield
+        o = jnp.concatenate([mm(pt[:RW], vs[0]), mm(pt[RW:], vs[1])], 0).astype(BF)
+        oi[j * LW:(j + 1) * LW] = o
+        out.extend([q, pb, ks, vs, o])
+        yield
+    def dense(i, os, out):
+        c0 = i * 2 * LW
+        g1v, b1v, g2v, b2v = [vec_ref[i] for i in range(2, 6)]
+        h = ht_ref[4 * i:4 * i + 4].reshape(2 * LW, DP)
+        o = jnp.concatenate(os, 0)
+        aT = mm_nt(woI_ref[...], jnp.concatenate([o, h], 1))
+        yield
+        n2, rc2, h2, hb2 = [], [], [], []
+        for t in range(2):
+            n, rc = norm_t(aT[:, t * LW:(t + 1) * LW])
+            hh = n * g1v + b1v
+            n2.append(n.astype(BF)); rc2.append(rc); hb2.append(hh.astype(BF))
+            yield
+        hb2 = jnp.concatenate(hb2, 1)
+        hb2T[:, c0:c0 + 2 * LW] = hb2
+        hb2 = tall(hb2)
+        C = CC
+        u = mm(w1T_ref[0:C], hb2)
+        for c in range(FF // C):
+            un = mm(w1T_ref[C * c + C:C * c + 2 * C], hb2) if c + 1 < FF // C else None
+            act, slope = gelu_parts(u.astype(BF))
+            acts[C * c:C * c + C, c0:c0 + 2 * LW] = act
+            slp[C * c:C * c + C, c0:c0 + 2 * LW] = slope
+            u = un
+            yield
+        gT = ct_ref[4 * i:4 * i + 4].reshape(2 * LW, DP).T[0:D].astype(F32)
+        z = mm(w2T_ref[...], acts[:, c0:c0 + 2 * LW])
+        yield
+        dbs, d3s = [], []
+        ys = []
+        for t in range(2):
+            sl = slice(t * LW, (t + 1) * LW)
+            n3, rc3 = norm_t(hb2[0:D, sl].astype(F32) + z[:, sl])
+            ys.append((n3 * g2v + b2v).astype(BF))
+            yield
+            g = gT[:, sl]
+            dnp[2] += g * n3
+            dnp[3] += g
+            d3 = norm_back_t(g, n3, rc3, g2v)
+            dbs.append(d3.astype(BF))
+            yield
+        db = jnp.concatenate(dbs, 1)
+        dbT[:, c0:c0 + 2 * LW] = db
+        db = tall(db)
+        w = mm(w2_ref[0:C], db)
+        for c in range(FF // C):
+            wn = mm(w2_ref[C * c + C:C * c + 2 * C], db) if c + 1 < FF // C else None
+            dus[C * c:C * c + C, c0:c0 + 2 * LW] = w.astype(BF) * slp[C * c:C * c + C, c0:c0 + 2 * LW]
+            w = wn
+            yield
+        dh = mm(w1_ref[...], dus[:, c0:c0 + 2 * LW])
+        yT = tall(jnp.concatenate(ys, 1))
+        y_ref[4 * i:4 * i + 4] = yT.T.reshape(4, RW, DP)
+        yield
+        dabs = []
+        for t in range(2):
+            dh2 = dbs[t].astype(F32) + dh[:, t * LW:(t + 1) * LW]
+            n2f = n2[t].astype(F32)
+            dnp[0] += dh2 * n2f
+            dnp[1] += dh2
+            dabs.append(norm_back_t(dh2, n2f, rc2[t], g1v).astype(BF))
+            yield
+        dab = jnp.concatenate(dabs, 1)
+        dabT[:, c0:c0 + 2 * LW] = dab
+        doT = mm(wo_ref[...], tall(dab)).astype(BF)
+        out.extend([dab, doT])
+        yield
+    def back(j, at, doT, out):
+        q, pb, ks, vs, _ = at
+        do = tall(doT)
+        don = do.T
+        dp = jnp.where(left, mm(vs[0], do), mm(vs[1], do))
+        yield
+        slot_sums(dv_ref, j, pb, don, None)
+        yield
+        dss = []
+        for hh in range(H):
+            sl = slice(hh * keys, (hh + 1) * keys)
+            p, d = pb[sl].astype(F32), dp[sl]
+            dss.append((p * (d - jnp.sum(p * d, 0, keepdims=True))).astype(BF))
+            if hh % 2: yield
+        ds = jnp.concatenate(dss, 0)
         dst = ds.T
-        dq = jnp.concatenate([mm(dst[:RW], ka), mm(dst[RW:], kb)], 0) * SCALE
-        dqs[pl.ds(s0, 2 * RW)] = dq.astype(BF)
+        yield
+        slot_sums(dk_ref, j, ds, q, 0.6931471805599453)
+        yield
+        dq = jnp.concatenate([mm(dst[:RW], ks[0]), mm(dst[RW:], ks[1])], 0) * SCALE
+        dq = dq.astype(BF)
+        dqs[j * LW:(j + 1) * LW] = dq
+        out.append(dq)
+        yield
+    lane = lax.broadcasted_iota(jnp.int32, (1, 128), 1)
+    zq = jnp.zeros((RW, 128), BF)
+    def slot_sums(ref, j, w, rows, scale):
+        out = [[], []]
+        for t, heads in ((0, 4), (1, 2)):
+            r = rows[:, 128 * t:128 * t + 128]
+            both = jnp.concatenate([jnp.concatenate([r[:RW], zq], 0), jnp.concatenate([zq, r[RW:]], 0)], 1)
+            full = mm(w[4 * t * keys:(4 * t + heads) * keys], both)
+            for c in range(2):
+                col = full[:, 128 * c:128 * c + 128]
+                v = col[0:keys]
+                for hh in range(1, heads):
+                    v = jnp.where(lane >= E * hh, col[hh * keys:(hh + 1) * keys], v)
+                out[c].append(v)
         for c in range(2):
-            part = slice(c * RW, (c + 1) * RW)
-            qz = jnp.concatenate([q[part], zero] if c == 0 else [zero, q[part]], 0)
-            dz = jnp.concatenate([do[part], zero] if c == 0 else [zero, do[part]], 0)
-            dk_ref[2 * j + c] = (diagonal(mm(ds, qz), keys) * SCALE).astype(BF)
-            dv_ref[2 * j + c] = diagonal(mm(pb, dz), keys).astype(BF)
-        return carry
-
-    lax.fori_loop(0, FB // 2, back, 0)
-
-    def finish(j, carry):
-        s0 = pl.multiple_of(j * CH, CH)
-        cols = CH // RW
-        g = da2s[pl.ds(s0, CH)] + mm(dqs[pl.ds(s0, CH)], wqT_ref[...])
-        g1_ref[pl.ds(j * cols, cols)] = g.astype(BF).reshape(cols, RW, DP)
-        return carry
-
-    lax.fori_loop(0, M // CH, finish, 0)
-    dwq[...] += mm_tn(h1b[...], dqs[...])
-    dwo[...] += mm_tn(oi[...], dab[...])
-    dw1[...] += mm_tn(h2b[...], dub[...])
-    dw2[...] += mm_tn(dbr[...], acts[...])
-
-    @pl.when(pl.program_id(0) == pl.num_programs(0) - 1)
-    def _():
-        at = 0
-        for ref in (dw1, dw2):
-            for j in range(FF // 128):
-                pack_ref[at : at + D] = ref[0:D, 128 * j : 128 * j + 128].astype(BF)
-                at += D
-        pack_pair(pack_ref, at, dwq, dwo)
-        pack_norms(pack_ref, at + PAIR, [dnp[i] for i in range(4)])
-
-
-def item_and_dense(nt, ct, kt, vt, bias, ws, np8, packed, FB=8, CH=128):
-    RW = nt.shape[1]
+            v = jnp.concatenate(out[c], 1)
+            ref[2 * j + c] = (v if scale is None else v * scale).astype(BF)
+    def finish(i, dqv, dab):
+        dq = jnp.concatenate(dqv, 0)
+        g1 = mm(dq, wqT_ref[...]) + tall(dab).T.astype(F32)
+        g1_ref[4 * i:4 * i + 4] = g1.astype(BF).reshape(4, RW, DP)
+        yield
+    def chunk(i):
+        at = [[], []]
+        ga, gb = attend(2 * i, at[0]), attend(2 * i + 1, at[1])
+        for _ in zip(ga, gb): yield
+        for _ in ga: yield
+        for _ in gb: yield
+        out = []
+        yield from dense(i, [at[0][4], at[1][4]], out)
+        dab, doT = out
+        dq = []
+        for t in range(2):
+            yield from back(2 * i + t, at[t], doT[:, t * LW:(t + 1) * LW], dq)
+        yield from finish(i, dq, dab)
+    def wgrad(b):
+        dwq[...] += mm(hbTs[b], dqss[b])
+        yield
+        dwo[...] += mm(dabTs[b], ois[b])
+        yield
+        for c in range(0, FF, WC):
+            dw1[c:c + WC] += mm_nt(duss[b, c:c + WC], hb2Ts[b])
+            yield
+        for c in range(0, FF, WC):
+            dw2[c:c + WC] += mm_nt(actss[b, c:c + WC], dbTs[b])
+            yield
+    NC = FB // 4
+    if True:
+        weave([(chunk(i), i * OFF, 1) for i in range(NC)] + [(wgrad(1 - cur), WP, 1)])
+        @pl.when(step == pl.num_programs(0) - 1)
+        def _():
+            for _ in wgrad(cur): pass
+            at = 0
+            for ref in (dw1, dw2):
+                t = ref[...].T
+                for j in range(FF // 128):
+                    pack_ref[at:at + D] = t[:, 128 * j:128 * j + 128].astype(BF)
+                    at += D
+            pack_pair(pack_ref, at, dwq, tall(dwo[...]).T)
+            pack_norms(pack_ref, at + PAIR, [dnp[i] for i in range(4)])
+
+
+def item_and_dense(ht, ct, kt, vt, bias, ws, vec, packed, FB=8, OFF=0, WP=20, CC=384, WC=384):
+    RW = ht.shape[1]
     keys = kt.shape[1]
     M = FB * RW
     cells = pl.BlockSpec((FB, RW, DP), lambda i: (i, 0, 0))
     slots = pl.BlockSpec((FB, keys, DP), lambda i: (i, 0, 0))
-    own = pltpu.VMEM((M, DP), BF)
-    wide = pltpu.VMEM((M, FF), BF)
+    accs = [(D, DP), (D, DP), (FF, D), (FF, D), (4, D, 128)]
+    kept = [(D, M), (M, DP), (D, M), (FF, M), (D, M), (FF, M), (D, M), (M, DP)]
     return pl.pallas_call(
-        functools.partial(item_kernel, FB, RW, keys, CH),
+        functools.partial(item_kernel, FB, RW, keys, OFF, WP, CC, WC),
         grid=(pl.cdiv(F, FB),),
-        in_specs=[cells, cells, slots, slots, whole(bias)] + [whole(w) for w in ws] + [whole(np8)],
+        in_specs=[cells, cells, slots, slots, whole(bias)] + [whole(w) for w in ws] + [whole(vec)],
         out_specs=[cells, cells, slots, slots, pl.BlockSpec((packed, 128), lambda i: (0, 0))],
         out_shape=[shape((FP, RW, DP))] * 2 + [shape((FP, keys, DP))] * 2 + [shape((packed, 128))],
-        scratch_shapes=[
-            pltpu.VMEM((DP, DP), F32),
-            pltpu.VMEM((DP, DP), F32),
-            pltpu.VMEM((DP, FF), F32),
-            pltpu.VMEM((DP, FF), F32),
-            pltpu.VMEM((4, 8, DP), F32),
-            own,
-            own,
-            pltpu.VMEM((FB // 2, H * keys, 2 * RW), BF),
-            own,
-            pltpu.VMEM((M, DP), F32),
-            own,
-            own,
-            own,
-            own,
-            wide,
-            own,
-            wide,
-        ],
+        scratch_shapes=[pltpu.VMEM(a, F32) for a in accs]
+        + [pltpu.VMEM((2,) + a, BF) for a in kept]
+        + [pltpu.VMEM((FF, M), BF)],
         compiler_params=params(),
-        cost_estimate=cost(180), name="item_and_dense",
-    )(nt, ct, kt, vt, bias, *ws, np8)
+        cost_estimate=cost(110),
+        name="item_and_dense",
+    )(ht, ct, kt, vt, bias, *ws, vec)
 
 
 def backward_kernel(R, U, SL, x_ref, qkv_ref, p_ref, of_ref, n_ref, g1t_ref, yt_ref, *rest):
@@ -805,13 +910,13 @@
     w = in_ref[...]
     in_n[...] = w - clipped(scaled(grad, col, row, mean), w, D * FF)
     grad = wide(6 * D)
-    hid_g[...] = grad.T
+    hid_g[...] = grad
     col, row = stats(grad, to_col(mm_ref[1:2, :]), mh_ref[1:2, :])
     mm_n[1:2, :] = to_row(col)
     mh_n[1:2, :] = row
     mean = jnp.sum(row, 1, keepdims=True) * (1.0 / FF)
     w = hid_ref[...]
-    update = (grad * lax.rsqrt(col) * lax.rsqrt(row * (1.0 / mean))).T
+    update = grad * lax.rsqrt(col) * lax.rsqrt(row * (1.0 / mean))
     hid_n[...] = w - clipped(update, w, D * FF)
 
     pieces = []
@@ -831,35 +936,41 @@
 
 
 def optimizer(mid, tail, *state):
-    proj, outw, w_in, w_out, norms, sr, sc, ms, hs, ns = state
-    order = [proj, outw, w_in, w_out, norms, proj, outw, w_in, w_out, norms, sr, sc, ms, hs, ns]
-    return pl.pallas_call(
+    proj, outw, w_in, w_outT, norms, sr, sc, ms, hs, ns = state
+    order = [proj, outw, w_in, w_outT, norms, proj, outw, w_in, w_outT, norms, sr, sc, ms, hs, ns]
+    outs = pl.pallas_call(
         optimizer_kernel,
         out_shape=[shape(a.shape, F32) for a in order],
         compiler_params=params(),
         cost_estimate=cost(8), name="optimizer",
     )(mid, tail, *state)
+    outs = list(outs)
+    for i in (3, 8):
+        outs[i] = outs[i].T
+    return outs
 
 
 def on_device(n, cells, cotangent, train_count, key_mask, train_order, *state):
-    proj, outw, w_in, w_out, norms = state[:5]
+    state = list(state)
+    state[3] = state[3].T
+    proj, outw, w_in, w_outT, norms = state[:5]
     x = cells[0]
     rows_here = x.shape[0]
     unit = 8 * n
     tail_rows = -(-TAIL // unit) * unit
     mid_rows = -(-MID // unit) * unit
     perm = perm_matrix()
-    (wqkv, wqkvT, wo, woT, wkv2, wk2T, wv2T, wq2, wq2T, wo2, wo2T, w1, w1T, w2, w2T, np8) = prepare(
-        proj, outw, w_in, w_out, norms
+    (wqkv, wqkvT, wo, woT, wkv2, wk2T, wv2T, wq2, wq2T, wo2I, wo2, w1T, w1, w2T, w2, np8, vec) = prepare(
+        proj, outw, w_in, w_outT, norms
     )
     own_kv = slot_keys(train_count, key_mask, train_order, x, wqkv, wo, wkv2, np8)
     shards = lax.axis_size("rows")
     kv = lax.all_gather(own_kv, "rows", axis=0, tiled=True)
-    nt, nn, qkv, p, of = feature_forward(x, wqkv, wo, perm)
+    ht, nn, qkv, p, of = feature_forward(x, wqkv, wo, np8, perm)
     ct = to_columns(cotangent[0], perm)
     kt, vt, bias = gathered_columns(kv, perm)
-    ws = (wq2, wq2T, wo2, wo2T, w1, w1T, w2, w2T)
-    yt, g1t, dk, dv, mid = item_and_dense(nt, ct, kt, vt, bias, ws, np8, mid_rows)
+    ws = (wq2, wq2T, wo2I, wo2, w1T, w1, w2T, w2)
+    yt, g1t, dk, dv, mid = item_and_dense(ht, ct, kt, vt, bias, ws, vec, mid_rows)
     parts = slot_parts(dk, dv, perm).reshape((shards,) + own_kv.shape)
     parts = lax.all_to_all(parts, "rows", 0, 0)
     mid = sum_over_devices(mid, n)

time: 461 us -> 333 us (0.72)
  Pallas kernels: 346 us -> 225 us
  local copies, waits for them, and re-layouts: 33 us -> 26.5 us
    pallas_call x1, Pallas kernels: 185 us -> 63.1 us  [item_and_dense(): pl.pallas_call(functools.partial(item_kernel, FB, RW, keys, OFF, WP, CC,...]
    unnamed x17 -> x14, local copies, waits for them, and re-layouts: 33 us -> 26.5 us
  transfers between devices with their start and end apart: 6 -> 6, of which waited for: 5 -> 5; matrix products, arithmetic and copies ran while one was open for 4% -> 6% of each run, Pallas kernels for 30% -> 41%
where the time goes in v3:
time: 333 us; the launch traced here: 332 us
  Pallas kernels  225 us (68%)
  waiting for transfers between devices  46.6 us (14%)
  local copies, waits for them, and re-layouts  26.5 us (8%)
  starting transfers between devices  19.2 us (6%)
  between operations  14.8 us (4%)
    pallas_call x2, Pallas kernels, feature_backward(): pl.pallas_call(functools.partial(backward_kernel, R, U, SL), grid=(rows /...  80.2 us
    pallas_call x1, Pallas kernels, item_and_dense(): pl.pallas_call(functools.partial(item_kernel, FB, RW, keys, OFF, WP, CC,...  63.1 us
    pallas_call x1, Pallas kernels, feature_forward(): pl.pallas_call(functools.partial(forward_kernel, R, U), grid=(rows // R,)...  44.4 us
    unnamed x14, local copies, waits for them, and re-layouts  26.5 us
    all_to_all x2, waiting for transfers between devices, sum_over_devices(): return lax.all_to_all(copies, axes, 0, 0).reshape(n * rows, 128)  20.4 us
    all_to_all x2, waiting for transfers between devices, sum_over_devices(): parts = lax.all_to_all(packed.reshape(n, rows, 128), axes, 0, 0)  12.8 us
    all_to_all x1, waiting for transfers between devices, on_device(): parts = lax.all_to_all(parts, 'rows', 0, 0)  10.5 us
    all_to_all x2, starting transfers between devices, sum_over_devices(): parts = lax.all_to_all(packed.reshape(n, rows, 128), axes, 0, 0)  9.57 us
  transfers between devices with their start and end apart: 6, of which 5 were waited for; matrix products, arithmetic and copies ran while one was open for 6% of the time, Pallas kernels for 41%

profile of v3, /device:TPU:0, one launch (start us, length us, event | category | flops | bytes accessed | tf_op | source)
XLA Modules:
  0.0 332.1 jit_solution(10533579148550103995)
XLA Ops:
  7.2 0.0 all-gather.2.cloned.1.call-start
  7.9 6.0 %copy.39 = bf16[1,64,119,192]{3,2,1,0:T(8,128)(2,1)} copy(bf16[1,64,119,192]{2,3,1,0:T(8,128)(2,1)} %param.16) | data formatting | bytes 5849088 | tf_op args[0]
  13.9 3.9 %weights.1 = (bf16[256,768]{1,0:T(8,128)(2,1)}, bf16[768,256]{1,0:T(8,128)(2,1)}, bf16[256,256]{1,0:T(8,128)(2,1)}, bf16[256,256]{1,0:T(8,128)(2,1)}, bf16[256,3...) custom-call(f32[6,192,192]{2,1,0:T(8,128)} %proj_ref.1, ...), custom_call_target="tpu_custom_call" | custom-call | flops 4400000000 | bytes 4000000 | tf_op jit(solution)/shard_map/weights/pallas_call | solution.py:175
  17.8 0.0 copy-start
  17.8 4.3 %slot_keys.1 = bf16[4,120,384]{2,1,0:T(8,128)(2,1)} custom-call(s32[1]{0:T(128)S(6)} %copy.45.count_ref, s32[1,4]{1,0:T(1,128)} %mask_ref.1, s32[1,4]{1,0:T(1,128)} %order_ref.1, bf16[64,119,192]{2,1,0:T(8,128)(2,1)} %bitcast.13, bf16[256,768]{1,0:T(8,128)(2,1)} %get-tuple-element.70.wqkv_ref, bf16[256,256]{1,0:T(8,128)(2,1)} %get-tuple-element.71.wo_ref, ...), custom_call_target="tpu_custom_call" | custom-call | flops 4400000000 | bytes 4000000 | tf_op jit(solution)/shard_map/slot_keys/pallas_call | solution.py:228
  22.1 0.0 all-gather.2.cloned.1.call-update
  22.1 0.0 copy-done
  22.1 5.0 %copy.40 = bf16[1,64,119,192]{3,2,1,0:T(8,128)(2,1)} copy(bf16[1,64,119,192]{2,3,1,0:T(8,128)(2,1)S(1)} %copy-done) | data formatting | bytes 5849088 | tf_op args[1]
  27.1 9.0 %to_columns.1.ct_ref = bf16[128,64,256]{2,1,0:T(8,128)(2,1)} custom-call(bf16[64,119,192]{2,1,0:T(8,128)(2,1)} %bitcast.18, bf16[256,256]{1,0:T(8,128)(2,1)} %constant.2.clone.perm_ref.rest_3_.rest_6_), custom_call_target="tpu_custom_call" | custom-call | flops 9900000256 | bytes 9000000 | tf_op jit(solution)/shard_map/to_columns/pallas_call | solution.py:321
  36.2 44.4 %feature_forward.1 = (bf16[128,64,256]{2,1,0:T(8,128)(2,1)}, bf16[64,128,256]{2,1,0:T(8,128)(2,1)}, bf16[64,128,768]{2,1,0:T(8,128)(2,1)}, bf16[64,128,768]{2,1,0:T(8,128)(2,1)}, bf16[64,128,256]{2,1,0:T(8,128)(2,1)}) custom-call(bf16[64,119,192]{2,1,0:T(8,128)(2,1)} %bitcast.14, bf16[256,768]{1,0:T(8,128)(2,1)} %get-tuple-element.70.wqkv_ref, ...), custom_call_target="tpu_custom_call" | custom-call | flops 48399998976 | bytes 44000000 | tf_op jit(solution)/shard_map/feature_forward/pallas_call | solution.py:282
  80.6 2.9 all-gather.2.cloned.1.call-done.kv_ref
  83.5 4.5 %gathered_columns.1 = (bf16[128,32,256]{2,1,0:T(8,128)(2,1)}, bf16[128,32,256]{2,1,0:T(8,128)(2,1)}, f32[32,128]{1,0:T(8,128)}) custom-call(bf16[32,120,384]{2,1,0:T(8,128)(2,1)} %all-gather.2.cloned.1.call-done.kv_ref, bf16[256,256]{1,0:T(8,128)(2,1)} %constant.2.clone.perm_ref.rest_3_.rest_6_), custom_call_target="tpu_custom_call" | custom-call | flops 4400000000 | bytes 4000000 | tf_op jit(solution)/shard_map/gathered_columns/pallas_call | solution.py:351
  88.0 63.1 %item_and_dense.1 = (bf16[128,64,256]{2,1,0:T(8,128)(2,1)}, bf16[128,64,256]{2,1,0:T(8,128)(2,1)}, bf16[128,32,256]{2,1,0:T(8,128)(2,1)}, bf16[128,32,256]{2,1,0:T(8,128)(2,1)}, bf16[3072,128]{1,0:T(8,128)(2,1)}) custom-call(bf16[128,64,256]{2,1,0:T(8,128)(2,1)} %get-tuple-element.77.ht_ref, bf16[128,64,256]{2,1,0:T(8,128)(2,1)} %to_columns.1.ct_ref, ...), custom_call_target="tpu_custom_call" | custom-call | flops 121000001536 | bytes 110000000 | tf_op jit(solution)/shard_map/item_and_dense/pallas_call | solution.py:656
  151.1 4.3 %slot_parts.1 = bf16[32,120,384]{2,1,0:T(8,128)(2,1)} custom-call(bf16[128,32,256]{2,1,0:T(8,128)(2,1)} %get-tuple-element.93.dk_ref, bf16[128,32,256]{2,1,0:T(8,128)(2,1)} %get-tuple-element.94.dv_ref, bf16[256,256]{1,0:T(8,128)(2,1)} %constant.2.clone.perm_ref.rest_3_.rest_6_), custom_call_target="tpu_custom_call" | custom-call | flops 4400000000 | bytes 4000000 | tf_op jit(solution)/shard_map/slot_parts/pallas_call | solution.py:381
  155.4 4.4 %all-to-all-start = ((bf16[8,4,120,384]{3,2,1,0:T(8,128)(2,1)}), bf16[8,4,120,384]{3,2,1,0:T(8,128)(2,1)S(1)}, u32[]{:S(2)}, u32[]{:S(2)}) async-start(bf16[8,4,120,384]{3,2,1,0:T(8,128)(2,1)} %bitcast.19), calls=%async_computation | async-start | bytes 5898240 | tf_op jit(solution)/shard_map/all_to_all | solution.py:975
  159.8 56.0 %feature_backward.2 = (f32[64,119,192]{2,1,0:T(8,128)}, bf16[64,119,192]{2,1,0:T(8,128)(2,1)}, f32[256,768]{1,0:T(8,128)}, f32[256,256]{1,0:T(8,128)}, f32[2,8,256]{2,1,0:T(8,128)}) custom-call(bf16[64,119,192]{2,1,0:T(8,128)(2,1)} %bitcast.15, bf16[64,128,768]{2,1,0:T(8,128)(2,1)} %get-tuple-element.73.qkv_ref, ...), custom_call_target="tpu_custom_call" | custom-call | flops 65999998976 | bytes 60000000 | tf_op jit(solution)/shard_map/feature_backward/pallas_call | solution.py:816
  215.7 10.5 %all-to-all-done.rest_0_ = bf16[8,4,120,384]{3,2,1,0:T(8,128)(2,1)S(1)} async-done(((bf16[8,4,120,384]{3,2,1,0:T(8,128)(2,1)}), bf16[8,4,120,384]{3,2,1,0:T(8,128)(2,1)S(1)}, u32[]{:S(2)}, u32[]{:S(2)}) %all-to-all-start) | async-done | bytes 2949152 | tf_op jit(solution)/shard_map/all_to_all | solution.py:975
  226.3 0.0 copy-start.1
  226.3 3.8 %all-to-all-start.1 = ((bf16[32,96,128]{2,1,0:T(8,128)(2,1)}), bf16[32,96,128]{2,1,0:T(8,128)(2,1)}, u32[]{:S(2)}, u32[]{:S(2)}) async-start(bf16[32,96,128]{2,1,0:T(8,128)(2,1)} %bitcast.20), calls=%async_computation.1 | async-start | bytes 1572864 | tf_op jit(solution)/shard_map/all_to_all | solution.py:841
  230.1 0.0 copy-done.1
  230.1 24.3 %feature_backward.3 = (f32[64,119,192]{2,1,0:T(8,128)}, bf16[64,119,192]{2,1,0:T(8,128)(2,1)}, bf16[1792,128]{1,0:T(8,128)(2,1)}) custom-call(bf16[64,119,192]{2,1,0:T(8,128)(2,1)} %bitcast.16, bf16[64,128,768]{2,1,0:T(8,128)(2,1)} %get-tuple-element.73.qkv_ref, ...), custom_call_target="tpu_custom_call", output_to_operand_aliasing={{0}: (17, {}), {1}: (18, {})} | custom-call | flops 65999998976 | bytes 60000000 | tf_op jit(solution)/shard_map/feature_backward/pallas_call | solution.py:816
  254.3 0.0 all-to-all-done.1.parts_ref
  254.4 5.8 %all-to-all-start.3 = ((bf16[32,56,128]{2,1,0:T(8,128)(2,1)}), bf16[32,56,128]{2,1,0:T(8,128)(2,1)S(1)}, u32[]{:S(2)}, u32[]{:S(2)}) async-start(bf16[32,56,128]{2,1,0:T(8,128)(2,1)} %bitcast.22), calls=%async_computation.3 | async-start | bytes 917504 | tf_op jit(solution)/shard_map/all_to_all | solution.py:841
  260.1 2.1 sum_parts.2
  262.3 12.8 %all-to-all-done.3.parts_ref = bf16[32,56,128]{2,1,0:T(8,128)(2,1)S(1)} async-done(((bf16[32,56,128]{2,1,0:T(8,128)(2,1)}), bf16[32,56,128]{2,1,0:T(8,128)(2,1)S(1)}, u32[]{:S(2)}, u32[]{:S(2)}) %all-to-all-start.3) | async-done | bytes 458784 | tf_op jit(solution)/shard_map/all_to_all | solution.py:841
  275.1 0.0 copy-start.4
  275.1 2.6 all-to-all-start.2
  277.7 0.0 copy-done.4
  277.7 1.9 sum_parts.3
  279.6 20.1 %all-to-all-done.2 = bf16[32,96,128]{2,1,0:T(8,128)(2,1)S(1)} async-done(((bf16[32,96,128]{2,1,0:T(8,128)(2,1)}), bf16[32,96,128]{2,1,0:T(8,128)(2,1)S(1)}, u32[]{:S(2)}, u32[]{:S(2)}) %all-to-all-start.2) | async-done | bytes 786464 | tf_op jit(solution)/shard_map/all_to_all | solution.py:845
  299.7 0.0 copy-start.2
  299.7 2.6 all-to-all-start.4
  302.3 6.0 %copy.41 = bf16[1,64,119,192]{2,3,1,0:T(8,128)(2,1)} copy(bf16[1,64,119,192]{3,2,1,0:T(8,128)(2,1)} %bitcast.17) | data formatting | bytes 5849088
  308.3 0.0 copy-done.2
  308.3 8.6 %copy.42 = f32[1,64,119,192]{2,3,1,0:T(8,128)} copy(f32[1,64,119,192]{3,2,1,0:T(8,128)} %bitcast.12) | data formatting | bytes 11698176
  317.0 0.3 all-to-all-done.4
  317.3 0.0 copy-start.3
  317.3 0.8 copy-done.3
  318.0 7.2 %optimizer.1 = (f32[6,192,192]{2,1,0:T(8,128)}, f32[2,192,192]{2,1,0:T(8,128)}, f32[192,768]{1,0:T(8,128)}, f32[192,768]{1,0:T(8,128)}, f32[6,192]{1,0:T(8,128)}...) custom-call(bf16[3072,128]{1,0:T(8,128)(2,1)} %bitcast.21, ...), custom_call_target="tpu_custom_call" | custom-call | flops 8800000000 | bytes 8000000 | tf_op jit(solution)/shard_map/optimizer/pallas_call | solution.py:941
Async XLA Ops:
  7.2 76.3 %all-gather.2.cloned.1.call-start = ((), (), s32[]{:S(2)}) async-start(), calls=%async_computation.5 | async-start | bytes 3317760 | tf_op jit(solution)/shard_map/all_gather | solution.py:968
  17.8 4.3 %copy-start = (bf16[1,64,119,192]{2,3,1,0:T(8,128)(2,1)S(1)}, bf16[1,64,119,192]{2,3,1,0:T(8,128)(2,1)}, u32[]{:S(2)}) copy-start(bf16[1,64,119,192]{2,3,1,0:T(8,128)(2,1)} %param.17) | copy-start | bytes 8773636
  155.4 70.9 %all-to-all-start = ((bf16[8,4,120,384]{3,2,1,0:T(8,128)(2,1)}), bf16[8,4,120,384]{3,2,1,0:T(8,128)(2,1)S(1)}, u32[]{:S(2)}, u32[]{:S(2)}) async-start(bf16[8,4,120,384]{3,2,1,0:T(8,128)(2,1)} %bitcast.19), calls=%async_computation | async-start | bytes 5898240 | tf_op jit(solution)/shard_map/all_to_all | solution.py:975
  226.3 3.8 %copy-start.1 = (bf16[8,4,120,384]{3,2,1,0:T(8,128)(2,1)}, bf16[8,4,120,384]{3,2,1,0:T(8,128)(2,1)S(1)}, u32[]{:S(2)}) copy-start(bf16[8,4,120,384]{3,2,1,0:T(8,128)(2,1)S(1)} %all-to-all-done.rest_0_) | copy-start | bytes 8847364
  226.3 28.1 %all-to-all-start.1 = ((bf16[32,96,128]{2,1,0:T(8,128)(2,1)}), bf16[32,96,128]{2,1,0:T(8,128)(2,1)}, u32[]{:S(2)}, u32[]{:S(2)}) async-start(bf16[32,96,128]{2,1,0:T(8,128)(2,1)} %bitcast.20), calls=%async_computation.1 | async-start | bytes 1572864 | tf_op jit(solution)/shard_map/all_to_all | solution.py:841
  254.4 20.7 %all-to-all-start.3 = ((bf16[32,56,128]{2,1,0:T(8,128)(2,1)}), bf16[32,56,128]{2,1,0:T(8,128)(2,1)S(1)}, u32[]{:S(2)}, u32[]{:S(2)}) async-start(bf16[32,56,128]{2,1,0:T(8,128)(2,1)} %bitcast.22), calls=%async_computation.3 | async-start | bytes 917504 | tf_op jit(solution)/shard_map/all_to_all | solution.py:841
  275.1 2.6 copy-start.4
  275.1 24.6 %all-to-all-start.2 = ((bf16[32,96,128]{2,1,0:T(8,128)(2,1)}), bf16[32,96,128]{2,1,0:T(8,128)(2,1)S(1)}, u32[]{:S(2)}, u32[]{:S(2)}) async-start(bf16[32,96,128]{2,1,0:T(8,128)(2,1)} %sum_parts.2), calls=%async_computation.2 | async-start | bytes 1572864 | tf_op jit(solution)/shard_map/all_to_all | solution.py:845
  299.7 8.6 %copy-start.2 = (bf16[32,96,128]{2,1,0:T(8,128)(2,1)}, bf16[32,96,128]{2,1,0:T(8,128)(2,1)S(1)}, u32[]{:S(2)}) copy-start(bf16[32,96,128]{2,1,0:T(8,128)(2,1)S(1)} %all-to-all-done.2) | copy-start | bytes 2359300
  299.7 17.6 %all-to-all-start.4 = ((bf16[32,56,128]{2,1,0:T(8,128)(2,1)}), bf16[32,56,128]{2,1,0:T(8,128)(2,1)S(1)}, u32[]{:S(2)}, u32[]{:S(2)}) async-start(bf16[32,56,128]{2,1,0:T(8,128)(2,1)} %sum_parts.3), calls=%async_computation.4 | async-start | bytes 917504 | tf_op jit(solution)/shard_map/all_to_all | solution.py:845
  317.3 0.8 copy-start.3
Sparse Core Ops, SparseCore 0:
  22.3 61.1 all-gather.1
